TPU v7x, 512 devices: a whole 4x4x16 slice. The times are simulated.
512 devices in a mesh: gx: 64 (over z, x_hi, core), gy: 8 (over x_lo, y).
Axes of the slice: x: 4 (x_hi: 2, x_lo: 2; x = x_hi * 2 + x_lo), y: 4, z: 16, core: 2. Of those that a mesh axis runs over, the one named last changes fastest.
Arguments:
- voxels: bfloat16 [64, 8, 8, 64, 128], P('gx', 'gy'), may hold values from -6 to 6
- first_weight: bfloat16 [27, 128, 128], replicated, may hold values from -0.21875 to 0.21875
- second_weight: bfloat16 [27, 128, 128], replicated, may hold values from -0.21875 to 0.21875
- in_slots: int32 [64, 8, 27, 2], P('gx', 'gy'), may hold values from 0 to 23
- out_slots: int32 [64, 8, 27, 2], P('gx', 'gy'), may hold values from 0 to 7
- live_slots: int32 [64, 8, 27, 2], P('gx', 'gy'), may hold values 0 or 1
- out_grad: bfloat16 [64, 8, 8, 64, 128], P('gx', 'gy'), may hold values from -6 to 6
Outputs:
- result: bfloat16 [64, 8, 8, 64, 128], P('gx', 'gy')
- input_grad: bfloat16 [64, 8, 8, 64, 128], P('gx', 'gy')
- first_grad: bfloat16 [27, 128, 128], replicated
- second_grad: bfloat16 [27, 128, 128], replicated
Inputs may be any that keep to these rules, and one draw needn't show every extreme that they name: `in_slots`: A value below 8 names the tile's own block; 8 + g * 2 + r names block r of the g-th neighbouring tile (3 x 3 neighbourhood in row-major order, centre skipped). A tile's blocks 0 to 1 are its boundary blocks. `out_slots`: output blocks always belong to the pair's own tile. `live_slots`: A slot with 0 holds no pair and contributes nothing.
All inputs are finite; a program needn't handle non-finite values. No bound on the sum of `live_slots` on one device may be relied on, other than what follows from the above.
Results may differ from a plain program's by a relative error of at most 0.0058.
Values may be sent and summed in bfloat16 or wider, within the bound.
A program may use at most 64 MiB of HBM per device.

v0:
```python
import math

import jax
import jax.numpy as jnp
from jax import lax
from jax.sharding import PartitionSpec as P

RIM = 2


def padded(block, sides, width):
    for axis, dim in sides:
        count = lax.axis_size(axis)
        forward = [(i, i + 1) for i in range(count - 1)]
        backward = [(target, source) for source, target in forward]
        low = lax.ppermute(
            lax.slice_in_dim(block, block.shape[dim] - width, None, axis=dim), axis, forward
        )
        high = lax.ppermute(lax.slice_in_dim(block, 0, width, axis=dim), axis, backward)
        block = jnp.concatenate([low, block, high], axis=dim)
    return block


def smooth_slope(values):
    sigmoid = jax.nn.sigmoid(values)
    return sigmoid * (1.0 + values * (1.0 - sigmoid))


def share_rim(local):
    depth = RIM
    edge = local[:depth][None, None]
    beside_all = padded(edge, (("gx", 0), ("gy", 1)), 1)
    beside_all = beside_all.reshape((9, depth) + local.shape[1:])
    lower = beside_all[:4].reshape((-1,) + local.shape[1:])
    upper = beside_all[5:].reshape((-1,) + local.shape[1:])
    return jnp.concatenate([local, lower, upper], axis=0)


def return_rim(table_grad, blocks):
    depth = RIM
    shape_tail = table_grad.shape[1:]
    remote = table_grad[blocks:].reshape((8, depth) + shape_tail)
    middle = jnp.zeros((1, depth) + shape_tail, jnp.float32)
    layout = jnp.concatenate([remote[:4], middle, remote[4:]], axis=0).reshape(
        (3, 3, depth) + shape_tail
    )
    along = padded(layout, (("gx", 0),), 1)
    column = along[0] + along[2] + along[4]
    across = padded(column, (("gy", 0),), 1)
    arrived = across[0] + across[2] + across[4]
    return table_grad[:blocks].at[:depth].add(arrived)


def convolve(table, in_rows, out_rows, live_rows, weight, blocks):
    offsets, slot_count = in_rows.shape
    voxel_count, width = (table.shape[1], table.shape[2])
    picked = jnp.take(table, in_rows.reshape(-1), axis=0).reshape(
        offsets, slot_count * voxel_count, width
    )
    product = jnp.einsum("kmc,kcd->kmd", picked, weight, preferred_element_type=jnp.float32)
    product = product.reshape(offsets * slot_count, voxel_count * width)
    targets = lax.broadcasted_iota(jnp.int32, (blocks, offsets * slot_count), 0)
    placing = ((out_rows.reshape(1, -1) == targets) & (live_rows.reshape(1, -1) > 0)).astype(
        jnp.float32
    )
    summed = jnp.dot(
        placing, product, precision=lax.Precision.HIGHEST, preferred_element_type=jnp.float32
    )
    return (summed.reshape(blocks, voxel_count, width), picked)


def transpose_conv(delta, picked, in_rows, out_rows, live_rows, weight, table_rows):
    offsets, slot_count = in_rows.shape
    voxel_count, width = (delta.shape[1], delta.shape[2])
    keep = live_rows.reshape(-1, 1, 1).astype(delta.dtype)
    gathered = (jnp.take(delta, out_rows.reshape(-1), axis=0) * keep).reshape(
        offsets, slot_count * voxel_count, width
    )
    backward = jnp.einsum("kmd,kcd->kmc", gathered, weight, preferred_element_type=jnp.float32)
    backward = backward.reshape(offsets * slot_count, voxel_count * width)
    sources = lax.broadcasted_iota(jnp.int32, (table_rows, offsets * slot_count), 0)
    placing = (in_rows.reshape(1, -1) == sources).astype(jnp.float32)
    table_grad = jnp.dot(
        placing, backward, precision=lax.Precision.HIGHEST, preferred_element_type=jnp.float32
    )
    weight_grad = jnp.einsum("kmc,kmd->kcd", picked, gathered, preferred_element_type=jnp.float32)
    return (table_grad.reshape(table_rows, voxel_count, width), weight_grad)


def shards(voxels, first_weight, second_weight, in_slots, out_slots, live_slots, out_grad):
    blocks = voxels.shape[2]
    shape_tail = voxels.shape[3:]
    inputs = voxels.reshape((blocks,) + shape_tail)
    cotangent = out_grad.reshape((blocks,) + shape_tail)
    in_rows = in_slots.reshape(in_slots.shape[2:])
    out_rows = out_slots.reshape(out_slots.shape[2:])
    live_rows = live_slots.reshape(live_slots.shape[2:])
    table_x = share_rim(inputs)
    table_rows = table_x.shape[0]
    first_sum, picked_x = convolve(table_x, in_rows, out_rows, live_rows, first_weight, blocks)
    hidden = jax.nn.silu(first_sum).astype(jnp.bfloat16)
    table_h = share_rim(hidden)
    second_sum, picked_h = convolve(table_h, in_rows, out_rows, live_rows, second_weight, blocks)
    joined = second_sum + inputs.astype(jnp.float32)
    result = jax.nn.silu(joined).astype(jnp.bfloat16)
    second_delta = (cotangent.astype(jnp.float32) * smooth_slope(joined)).astype(jnp.bfloat16)
    grads_h, second_grad = transpose_conv(
        second_delta, picked_h, in_rows, out_rows, live_rows, second_weight, table_rows
    )
    hidden_grad = return_rim(grads_h, blocks)
    first_delta = (hidden_grad * smooth_slope(first_sum)).astype(jnp.bfloat16)
    grads_x, first_grad = transpose_conv(
        first_delta, picked_x, in_rows, out_rows, live_rows, first_weight, table_rows
    )
    first_grad, second_grad = lax.psum((first_grad, second_grad), ("gx", "gy"))
    input_grad = return_rim(grads_x, blocks) + second_delta.astype(jnp.float32)
    scale = 1.0 / math.sqrt(
        lax.axis_size("gx")
        * lax.axis_size("gy")
        * in_rows.shape[0]
        * in_rows.shape[1]
        * shape_tail[0]
    )
    return (
        result.reshape(voxels.shape),
        input_grad.astype(jnp.bfloat16).reshape(voxels.shape),
        (first_grad * scale).astype(jnp.bfloat16),
        (second_grad * scale).astype(jnp.bfloat16),
    )


def solution(mesh):
    return jax.shard_map(
        shards,
        mesh=mesh,
        in_specs=(
            P("gx", "gy", None, None, None),
            P(),
            P(),
            P("gx", "gy", None, None),
            P("gx", "gy", None, None),
            P("gx", "gy", None, None),
            P("gx", "gy", None, None, None),
        ),
        out_specs=(P("gx", "gy", None, None, None), P("gx", "gy", None, None, None), P(), P()),
        check_vma=False,
    )
```

profile of v0, /device:TPU:1, one launch (start us, length us, event | category | flops | bytes accessed | tf_op | source)
XLA Modules:
  0.0 619.7 jit_solution(6861861382084516616)
XLA Ops:
  8.1 8.8 %collective-permute-start.1 = (bf16[1,1,2,64,128]{4,3,2,1,0:T(8,128)(2,1)S(1)}, bf16[1,1,2,64,128]{4,3,2,1,0:T(8,128)(2,1)S(1)}, u32[]{:S(2)}, u32[]{:S(2)}) collective-permute-start(bf16[1,1,2,64,128]{4,3,2,1,0:T(8,128)(2,1)S(1)} %slice.177), channel_id=1, source_target_pairs={{8,0},{16,8},{24,16},{32,24},{40,32},{48,40},{56,48},{64,56},{72,6... | collective-permute-start | bytes 98312 | tf_op jit(solution)/shard_map/ppermute | solution.py:19
  16.8 1.9 collective-permute-start
  24.8 4.0 collective-permute-start.2
  33.2 1.6 reshape.204
  34.8 1.8 copy.59
  36.9 2.4 multiply_convert_fusion.4
  39.3 3.5 collective-permute-start.5
  42.9 3.5 collective-permute-start.4
  49.3 4.5 collective-permute-start.6
  54.1 1.8 collective-permute-done.6
  58.5 1.6 fusion.43
  60.1 2.7 reshape.209
  62.8 1.8 copy.60
  65.6 2.5 fusion.7
  68.8 1.6 gather_fusion.2
  71.7 2.0 fusion.44
  73.7 2.7 reshape.212
  76.4 2.2 fusion.23
  78.9 2.0 collective-permute-start.9
  81.1 5.4 collective-permute-start.8
  87.8 2.6 collective-permute-done.8
  91.9 4.8 collective-permute-start.10
  96.7 1.7 fusion.47
  101.6 2.0 fusion.45
  103.6 1.7 fusion.46
  105.3 1.6 reshape.215
  107.9 1.9 collective-permute-start.13
  110.1 6.3 %collective-permute-start.12 = (f32[1,3,2,64,128]{4,2,3,1,0:T(2,128)S(1)}, f32[1,3,2,64,128]{4,2,3,1,0:T(2,128)S(1)}, u32[]{:S(2)}, u32[]{:S(2)}) collective-permute-start(f32[1,3,2,64,128]{4,2,3,1,0:T(2,128)S(1)} %copy.45), channel_id=1, source_target_pairs={{0,8},{8,16},{16,24},{24,32},{32,40},{40,48},{48,56},{56,64},{64,7... | collective-permute-start | bytes 589832 | tf_op jit(solution)/shard_map/ppermute | solution.py:16
  117.6 2.3 collective-permute-done.12
  121.4 4.6 collective-permute-start.14
  128.1 480.8 %all-reduce.3.cloned.1.call-done = (f32[27,128,128]{2,1,0:T(8,128)}, f32[27,128,128]{2,1,0:T(8,128)}) async-done(((f32[27,128,128]{2,1,0:T(8,128)}, f32[27,128,128]{2,1,0:T(8,128)}), (f32[27,128,128]{2,1,0:T(8,128)}, f32[27,128,128]{2,1,0:T(8,128)})) %all-reduce.3.cloned.1.call-update) | async-done | bytes 3538960 | tf_op jit(solution)/shard_map/psum | solution.py:115
  608.9 2.8 multiply_convert_fusion.1
  (134 shorter events, 33.4 us)
Async XLA Ops:
  7.2 51.3 %copy-start = (bf16[27,128,128]{2,1,0:T(8,128)(2,1)S(1)}, bf16[27,128,128]{2,1,0:T(8,128)(2,1)}, u32[]{:S(2)}) copy-start(bf16[27,128,128]{2,1,0:T(8,128)(2,1)} %param.17) | copy-start | bytes 2654212
  7.2 601.7 %all-reduce.3.cloned.1.call-start = ((), (), s32[]{:S(2)}) async-start(), calls=%async_computation | async-start | bytes 7077888 | tf_op jit(solution)/shard_map/psum | solution.py:115
  8.1 15.4 %collective-permute-start.1 = (bf16[1,1,2,64,128]{4,3,2,1,0:T(8,128)(2,1)S(1)}, bf16[1,1,2,64,128]{4,3,2,1,0:T(8,128)(2,1)S(1)}, u32[]{:S(2)}, u32[]{:S(2)}) collective-permute-start(bf16[1,1,2,64,128]{4,3,2,1,0:T(8,128)(2,1)S(1)} %slice.177), channel_id=1, source_target_pairs={{8,0},{16,8},{24,16},{32,24},{40,32},{48,40},{56,48},{64,56},{72,6... | collective-permute-start | bytes 98312 | tf_op jit(solution)/shard_map/ppermute | solution.py:19
  16.8 6.6 %collective-permute-start = (bf16[1,1,2,64,128]{4,3,2,1,0:T(8,128)(2,1)S(1)}, bf16[1,1,2,64,128]{4,3,2,1,0:T(8,128)(2,1)S(1)}, u32[]{:S(2)}, u32[]{:S(2)}) collective-permute-start(bf16[1,1,2,64,128]{4,3,2,1,0:T(8,128)(2,1)S(1)} %slice.177), channel_id=1, source_target_pairs={{0,8},{8,16},{16,24},{24,32},{32,40},{40,48},{48,56},{56,64},{64,7... | collective-permute-start | bytes 98312 | tf_op jit(solution)/shard_map/ppermute | solution.py:16
  21.6 10.1 %copy-start.14 = (pred[54]{0:T(512)(128)(4,1)}, pred[54]{0:T(512)(128)(4,1)S(1)}, u32[]{:S(2)}) copy-start(pred[54]{0:T(512)(128)(4,1)S(1)} %get-tuple-element.65) | copy-start | bytes 166
  23.5 13.4 %copy-start.12 = (pred[54]{0:T(512)(128)(4,1)}, pred[54]{0:T(512)(128)(4,1)S(1)}, u32[]{:S(2)}) copy-start(pred[54]{0:T(512)(128)(4,1)S(1)} %gt.13) | copy-start | bytes 166
  23.5 5.8 collective-permute-start.3
  24.8 5.6 collective-permute-start.2
  31.7 1.2 copy-start.1
  36.9 9.5 %copy-start.18 = (s32[1,1,27,2]{2,3,1,0:T(2,128)S(1)}, s32[1,1,27,2]{2,3,1,0:T(2,128)}, u32[]{:S(2)}) copy-start(s32[1,1,27,2]{2,3,1,0:T(2,128)} %param.20) | copy-start | bytes 652
  36.9 17.0 %copy-start.17 = (s32[54]{0:T(128)S(1)}, s32[54]{0:T(128)}, u32[]{:S(2)}) copy-start(s32[54]{0:T(128)} %get-tuple-element.62) | copy-start | bytes 652
  39.3 8.5 %collective-permute-start.5 = (bf16[1,1,2,64,128]{4,2,3,1,0:T(2,128)(2,1)S(1)}, bf16[1,1,2,64,128]{4,2,3,1,0:T(2,128)(2,1)S(1)}, u32[]{:S(2)}, u32[]{:S(2)}) collective-permute-start(bf16[1,1,2,64,128]{4,2,3,1,0:T(2,128)(2,1)S(1)} %slice_bitcast_fusion.14), channel_id=1, source_target_pairs={{8,0},{16,8},{24,16},{32,24},{40,32},{48,40},{56,48},{64,56},{72,6... | collective-permute-start | bytes 98312 | tf_op jit(solution)/shard_map/ppermute | solution.py:19
  42.9 5.0 collective-permute-start.4
  48.0 6.1 collective-permute-start.7
  49.3 6.6 %collective-permute-start.6 = (bf16[3,1,2,64,128]{4,2,3,1,0:T(2,128)(2,1)S(1)}, bf16[3,1,2,64,128]{4,2,3,1,0:T(2,128)(2,1)S(1)}, u32[]{:S(2)}, u32[]{:S(2)}) collective-permute-start(bf16[3,1,2,64,128]{4,2,3,1,0:T(2,128)(2,1)S(1)} %pad_maximum_fusion.9), channel_id=1, source_target_pairs={{0,1},{1,2},{2,3},{3,4},{4,5},{5,6},{6,7},{8,9},{9,10},{10,11},{11... | collective-permute-start | bytes 294920 | tf_op jit(solution)/shard_map/ppermute | solution.py:16
  65.6 4.8 copy-start.10
  68.1 2.3 copy-start.11
  78.9 8.9 %collective-permute-start.9 = (f32[1,3,2,64,128]{4,2,3,1,0:T(2,128)S(1)}, f32[1,3,2,64,128]{4,2,3,1,0:T(2,128)S(1)}, u32[]{:S(2)}, u32[]{:S(2)}) collective-permute-start(f32[1,3,2,64,128]{4,2,3,1,0:T(2,128)S(1)} %copy.43), channel_id=1, source_target_pairs={{8,0},{16,8},{24,16},{32,24},{40,32},{48,40},{56,48},{64,56},{72,6... | collective-permute-start | bytes 589832 | tf_op jit(solution)/shard_map/ppermute | solution.py:19
  81.1 9.2 %copy-start.15 = (f32[3]{0:T(128)S(1)}, f32[3]{0:T(128)}, u32[]{:S(2)}) copy-start(f32[3]{0:T(128)} %slice.231) | copy-start | bytes 40
  81.1 9.2 %collective-permute-start.8 = (f32[1,3,2,64,128]{4,2,3,1,0:T(2,128)S(1)}, f32[1,3,2,64,128]{4,2,3,1,0:T(2,128)S(1)}, u32[]{:S(2)}, u32[]{:S(2)}) collective-permute-start(f32[1,3,2,64,128]{4,2,3,1,0:T(2,128)S(1)} %copy.40), channel_id=1, source_target_pairs={{0,8},{8,16},{16,24},{24,32},{32,40},{40,48},{48,56},{56,64},{64,7... | collective-permute-start | bytes 589832 | tf_op jit(solution)/shard_map/ppermute | solution.py:16
  90.5 7.8 %collective-permute-start.11 = (f32[1,2,64,128]{3,1,2,0:T(2,128)S(1)}, f32[1,2,64,128]{3,1,2,0:T(2,128)S(1)}, u32[]{:S(2)}, u32[]{:S(2)}) collective-permute-start(f32[1,2,64,128]{3,1,2,0:T(2,128)S(1)} %get-tuple-element.59), channel_id=1, source_target_pairs={{1,0},{2,1},{3,2},{4,3},{5,4},{6,5},{7,6},{9,8},{10,9},{11,10},{12... | collective-permute-start | bytes 196616 | tf_op jit(solution)/shard_map/ppermute | solution.py:19
  91.8 6.6 %copy-start.6 = (f32[8,64,128]{2,0,1:T(8,128)S(1)}, f32[8,64,128]{2,0,1:T(8,128)}, u32[]{:S(2)}) copy-start(f32[8,64,128]{2,0,1:T(8,128)} %get-tuple-element.61) | copy-start | bytes 786436
  91.9 6.5 %collective-permute-start.10 = (f32[1,2,64,128]{3,1,2,0:T(2,128)S(1)}, f32[1,2,64,128]{3,1,2,0:T(2,128)S(1)}, u32[]{:S(2)}, u32[]{:S(2)}) collective-permute-start(f32[1,2,64,128]{3,1,2,0:T(2,128)S(1)} %get-tuple-element.58), channel_id=1, source_target_pairs={{0,1},{1,2},{2,3},{3,4},{4,5},{5,6},{6,7},{8,9},{9,10},{10,11},{11... | collective-permute-start | bytes 196616 | tf_op jit(solution)/shard_map/ppermute | solution.py:16
  98.6 3.0 copy-start.2
  107.9 9.7 %collective-permute-start.13 = (f32[1,3,2,64,128]{4,2,3,1,0:T(2,128)S(1)}, f32[1,3,2,64,128]{4,2,3,1,0:T(2,128)S(1)}, u32[]{:S(2)}, u32[]{:S(2)}) collective-permute-start(f32[1,3,2,64,128]{4,2,3,1,0:T(2,128)S(1)} %copy.48), channel_id=1, source_target_pairs={{8,0},{16,8},{24,16},{32,24},{40,32},{48,40},{56,48},{64,56},{72,6... | collective-permute-start | bytes 589832 | tf_op jit(solution)/shard_map/ppermute | solution.py:19
  110.0 9.8 %copy-start.16 = (f32[3]{0:T(128)S(1)}, f32[3]{0:T(128)}, u32[]{:S(2)}) copy-start(f32[3]{0:T(128)} %slice.231) | copy-start | bytes 40
  110.1 9.8 %collective-permute-start.12 = (f32[1,3,2,64,128]{4,2,3,1,0:T(2,128)S(1)}, f32[1,3,2,64,128]{4,2,3,1,0:T(2,128)S(1)}, u32[]{:S(2)}, u32[]{:S(2)}) collective-permute-start(f32[1,3,2,64,128]{4,2,3,1,0:T(2,128)S(1)} %copy.45), channel_id=1, source_target_pairs={{0,8},{8,16},{16,24},{24,32},{32,40},{40,48},{48,56},{56,64},{64,7... | collective-permute-start | bytes 589832 | tf_op jit(solution)/shard_map/ppermute | solution.py:16
  116.5 9.6 %copy-start.8 = (bf16[1,1,8,64,128]{4,2,3,1,0:T(8,128)(2,1)S(1)}, bf16[1,1,8,64,128]{4,2,3,1,0:T(8,128)(2,1)}, u32[]{:S(2)}) copy-start(bf16[1,1,8,64,128]{4,2,3,1,0:T(8,128)(2,1)} %get-tuple-element.55) | copy-start | bytes 393220
  116.5 10.9 %copy-start.5 = (bf16[8,64,128]{2,0,1:T(8,128)(2,1)S(1)}, bf16[8,64,128]{2,0,1:T(8,128)(2,1)}, u32[]{:S(2)}) copy-start(bf16[8,64,128]{2,0,1:T(8,128)(2,1)} %copy-done.4) | copy-start | bytes 393220
  120.1 6.6 %collective-permute-start.15 = (f32[1,2,64,128]{3,1,2,0:T(2,128)S(1)}, f32[1,2,64,128]{3,1,2,0:T(2,128)S(1)}, u32[]{:S(2)}, u32[]{:S(2)}) collective-permute-start(f32[1,2,64,128]{3,1,2,0:T(2,128)S(1)} %get-tuple-element.57), channel_id=1, source_target_pairs={{1,0},{2,1},{3,2},{4,3},{5,4},{6,5},{7,6},{9,8},{10,9},{11,10},{12... | collective-permute-start | bytes 196616 | tf_op jit(solution)/shard_map/ppermute | solution.py:19
  121.4 5.9 collective-permute-start.14
  608.9 2.8 copy-start.3
  (4 other events, 3.5 us)
Sparse Core Ops, SparseCore 0:
  107.0 501.8 all-reduce.2
where the time goes:
time: 621 us; the launch traced here: 620 us
  waiting for transfers between devices  491 us (79%)
  starting transfers between devices  56.6 us (9%)
  local copies, waits for them, and re-layouts  29.1 us (5%)
  matrix products  17.2 us (3%)
  between operations  14.8 us (2%)
  other arithmetic  10.9 us (2%)
    psum x1, waiting for transfers between devices, shards(): first_grad, second_grad = lax.psum((first_grad, second_grad), ('gx', 'gy'))  481 us
    ppermute x8, starting transfers between devices, padded(): lax.ppermute(lax.slice_in_dim(block, block.shape[dim] - width, None, axis...  35.2 us
    ppermute x8, starting transfers between devices, padded(): lax.ppermute(lax.slice_in_dim(block, 0, width, axis=dim), axis, backward)  21.4 us
  transfers between devices with their start and end apart: 17, of which 10 were waited for; matrix products, arithmetic and copies ran while one was open for 2% of the time, Pallas kernels for 0%

commit v1 on v0

--- a/solution.py
+++ b/solution.py
@@ -1,11 +1,336 @@
+import functools
 import math
 
 import jax
 import jax.numpy as jnp
 from jax import lax
+from jax.experimental import pallas as pl
+from jax.experimental.pallas import tpu as pltpu
 from jax.sharding import PartitionSpec as P
 
 RIM = 2
+MESH = pl.DeviceIdType.MESH
+
+ROWS = 27 * 128
+HALF = 1792
+FULL = 2 * HALF
+A_ROWS = 1024
+B_ROWS = 768
+A1, A2 = A_ROWS // 4, A_ROWS // 16
+B1, B2 = B_ROWS // 4, B_ROWS // 16
+TILES = (A2 + B2) // 16
+OWNER_BASE = (0, 8)
+
+
+def rows(start, size):
+    return pl.ds(pl.multiple_of(start, 16), size)
+
+
+def place():
+    gx, gy = lax.axis_index("gx"), lax.axis_index("gy")
+    core = lax.rem(gx, 2)
+    x = lax.rem(gx // 2, 2) * 2 + gy // 4
+    return gx // 4, x, lax.rem(gy, 4), core
+
+
+def device(z, x, y, core):
+    return ((z * 2 + x // 2) * 2 + core, lax.rem(x, 2) * 4 + y)
+
+
+def group_peers():
+    z, x, y, core = place()
+    peers = [device(z, x, y, 1 - core)]
+    peers += [device(z, x, lax.rem(y + d, 4), core) for d in (1, 2, 3)]
+    peers += [device(z, lax.rem(x + d, 4), y, core) for d in (1, 2, 3)]
+    return peers
+
+
+class Reduce:
+    scratch = [
+        pltpu.VMEM((HALF, 128), jnp.bfloat16),
+        pltpu.VMEM((HALF, 128), jnp.bfloat16),
+        pltpu.VMEM((3, A1, 128), jnp.bfloat16),
+        pltpu.VMEM((3, B1, 128), jnp.bfloat16),
+        pltpu.VMEM((A1 + B1, 128), jnp.bfloat16),
+        pltpu.VMEM((3, A2, 128), jnp.bfloat16),
+        pltpu.VMEM((3, B2, 128), jnp.bfloat16),
+        pltpu.VMEM((A2 + B2, 128), jnp.bfloat16),
+        pltpu.VMEM((16, 16, 128), jnp.bfloat16),
+        pltpu.SemaphoreType.DMA((2, 28)),
+        pltpu.SemaphoreType.DMA((2, 16)),
+        pltpu.SemaphoreType.DMA((2, 16)),
+    ]
+
+    def __init__(self, index, part, out, scale, *scratch):
+        self.base, self.part, self.out, self.scale = OWNER_BASE[index], part, out, scale
+        (
+            self.got_core,
+            self.sum_core,
+            self.got_a1,
+            self.got_b1,
+            self.sum_1,
+            self.got_a2,
+            self.got_b2,
+            self.sum_2,
+            self.got_z,
+            self.sems,
+            self.to_owner,
+            self.from_owner,
+        ) = scratch
+        self.z, self.x, self.y, self.core = place()
+        self.sent = []
+
+    def send(self, src, dst, sem, device_id):
+        copy = pltpu.make_async_remote_copy(
+            src_ref=src,
+            dst_ref=dst,
+            send_sem=self.sems.at[0, sem],
+            recv_sem=self.sems.at[1, sem],
+            device_id=device_id,
+            device_id_type=MESH,
+        )
+        copy.start()
+        self.sent.append(copy)
+        return copy
+
+    def along(self, axis, d):
+        if axis == "y":
+            return device(self.z, self.x, lax.rem(self.y + d, 4), self.core)
+        return device(self.z, lax.rem(self.x + d, 4), self.y, self.core)
+
+    def at(self, axis, d):
+        return lax.rem((self.y if axis == "y" else self.x) + d, 4)
+
+    def start_core(self):
+        other = 1 - self.core
+        self.wait_core = self.send(
+            self.part.at[rows(other * HALF, HALF)],
+            self.got_core,
+            0,
+            device(self.z, self.x, self.y, other),
+        )
+
+    def scatter(self, src, offset, size, got, axis, sem):
+        return [
+            self.send(
+                src.at[rows(offset + self.at(axis, d) * size, size)],
+                got.at[d - 1],
+                sem + d,
+                self.along(axis, d),
+            )
+            for d in (1, 2, 3)
+        ]
+
+    def start_first(self):
+        self.wait_core.wait_recv()
+        own = self.part[rows(self.core * HALF, HALF)]
+        self.sum_core[...] = (
+            own.astype(jnp.float32) + self.got_core[...].astype(jnp.float32)
+        ).astype(jnp.bfloat16)
+        self.wait_a = self.scatter(self.sum_core, 0, A1, self.got_a1, "y", 0)
+        self.wait_b = self.scatter(self.sum_core, A_ROWS, B1, self.got_b1, "x", 3)
+
+    def gathered(self, own, got):
+        total = own.astype(jnp.float32)
+        for d in range(3):
+            total = total + got[d].astype(jnp.float32)
+        return total.astype(jnp.bfloat16)
+
+    def start_second(self):
+        for copy in self.wait_a:
+            copy.wait_recv()
+        self.sum_1[:A1] = self.gathered(self.sum_core[rows(self.y * A1, A1)], self.got_a1)
+        wait_a = self.scatter(self.sum_1, 0, A2, self.got_a2, "x", 6)
+        for copy in self.wait_b:
+            copy.wait_recv()
+        self.sum_1[A1:] = self.gathered(
+            self.sum_core[rows(A_ROWS + self.x * B1, B1)], self.got_b1
+        )
+        self.wait_b = self.scatter(self.sum_1, A1, B2, self.got_b2, "y", 9)
+        self.wait_a = wait_a
+
+    def owner_copy(self, tile):
+        owner = self.base + tile
+        d = lax.rem(owner - self.z + 16, 16)
+        return pltpu.make_async_remote_copy(
+            src_ref=self.sum_2.at[rows(tile * 16, 16)],
+            dst_ref=self.got_z.at[d],
+            send_sem=self.to_owner.at[0, d],
+            recv_sem=self.to_owner.at[1, d],
+            device_id=device(owner, self.x, self.y, self.core),
+            device_id_type=MESH,
+        )
+
+    def start_owner(self):
+        for copy in self.wait_a:
+            copy.wait_recv()
+        self.sum_2[:A2] = self.gathered(self.sum_1[rows(self.x * A2, A2)], self.got_a2)
+        for copy in self.wait_b:
+            copy.wait_recv()
+        self.sum_2[A2:] = self.gathered(self.sum_1[rows(A1 + self.y * B2, B2)], self.got_b2)
+
+        @pl.loop(0, TILES)
+        def _(tile):
+            @pl.when(self.base + tile != self.z)
+            def _():
+                self.owner_copy(tile).start()
+
+    def spot(self, tile):
+        a = self.core * HALF + self.y * A1 + self.x * A2 + tile * 16
+        b = self.core * HALF + A_ROWS + self.x * B1 + self.y * B2 + (tile - A2 // 16) * 16
+        first = tile < A2 // 16
+        return jnp.where(first, a, b)
+
+    def result_copy(self, tile, d):
+        piece = self.out.at[rows(self.spot(tile), 16)]
+        return pltpu.make_async_remote_copy(
+            src_ref=piece,
+            dst_ref=piece,
+            send_sem=self.from_owner.at[0, d],
+            recv_sem=self.from_owner.at[1, tile],
+            device_id=device(lax.rem(self.z + d, 16), self.x, self.y, self.core),
+            device_id_type=MESH,
+        )
+
+    def owned(self):
+        return (self.z >= self.base) & (self.z < self.base + TILES)
+
+    def start_result(self):
+        @pl.when(self.owned())
+        def _():
+            tile = self.z - self.base
+
+            @pl.loop(1, 16)
+            def _(d):
+                pltpu.make_async_copy(
+                    self.got_z.at[d], self.got_z.at[d], self.to_owner.at[1, d]
+                ).wait()
+
+            total = self.sum_2[rows(tile * 16, 16)].astype(jnp.float32)
+            for d in range(1, 16):
+                total = total + self.got_z[d].astype(jnp.float32)
+            self.out[rows(self.spot(tile), 16)] = (total * self.scale).astype(jnp.bfloat16)
+
+            @pl.loop(1, 16)
+            def _(d):
+                self.result_copy(tile, d).start()
+
+    def gather(self, offset, size, axis, sem):
+        piece = self.out.at[rows(offset + self.at(axis, 0) * size, size)]
+        for d in (1, 2, 3):
+            self.send(piece, piece, sem + d, self.along(axis, d))
+
+    def wait_gather(self, offset, size, axis, sem):
+        for d in (1, 2, 3):
+            piece = self.out.at[rows(offset + self.at(axis, 4 - d) * size, size)]
+            pltpu.make_async_copy(piece, piece, self.sems.at[1, sem + d]).wait()
+
+    def start_gather_second(self):
+        @pl.loop(0, TILES)
+        def _(tile):
+            @pl.when(self.base + tile != self.z)
+            def _():
+                piece = self.out.at[rows(self.spot(tile), 16)]
+                pltpu.make_async_copy(piece, piece, self.from_owner.at[1, tile]).wait()
+
+        half = self.core * HALF
+        self.gather(half + self.y * A1, A2, "x", 12)
+        self.gather(half + A_ROWS + self.x * B1, B2, "y", 15)
+
+    def start_gather_first(self):
+        half = self.core * HALF
+        self.wait_gather(half + self.y * A1, A2, "x", 12)
+        self.gather(half, A1, "y", 18)
+        self.wait_gather(half + A_ROWS + self.x * B1, B2, "y", 15)
+        self.gather(half + A_ROWS, B1, "x", 21)
+
+    def start_gather_core(self):
+        half = self.core * HALF
+        self.wait_gather(half, A1, "y", 18)
+        self.wait_gather(half + A_ROWS, B1, "x", 21)
+        other = device(self.z, self.x, self.y, 1 - self.core)
+        piece = self.out.at[rows(half, HALF)]
+        self.send(piece, piece, 25, other)
+
+    def finish(self):
+        piece = self.out.at[rows((1 - self.core) * HALF, HALF)]
+        pltpu.make_async_copy(piece, piece, self.sems.at[1, 25]).wait()
+        for copy in self.sent:
+            copy.wait_send()
+
+        @pl.loop(0, TILES)
+        def _(tile):
+            @pl.when(self.base + tile != self.z)
+            def _():
+                self.owner_copy(tile).wait_send()
+
+        @pl.when(self.owned())
+        def _():
+            @pl.loop(1, 16)
+            def _(d):
+                self.result_copy(self.z - self.base, d).wait_send()
+
+
+def enter(peers):
+    barrier = pltpu.get_barrier_semaphore()
+    for peer in peers:
+        pl.semaphore_signal(barrier, inc=1, device_id=peer, device_id_type=MESH)
+    z, x, y, core = place()
+
+    @pl.loop(1, 16)
+    def _(d):
+        pl.semaphore_signal(
+            barrier,
+            inc=1,
+            device_id=device(lax.rem(z + d, 16), x, y, core),
+            device_id_type=MESH,
+        )
+
+    pl.semaphore_wait(barrier, len(peers) + 15)
+
+
+def reduce_kernel(scale, first_part, second_part, first_out, second_out, *scratch):
+    enter(group_peers())
+    count = len(Reduce.scratch)
+    both = [
+        Reduce(0, first_part, first_out, scale, *scratch[:count]),
+        Reduce(1, second_part, second_out, scale, *scratch[count:]),
+    ]
+    for step in (
+        "start_core",
+        "start_first",
+        "start_second",
+        "start_owner",
+        "start_result",
+        "start_gather_second",
+        "start_gather_first",
+        "start_gather_core",
+        "finish",
+    ):
+        for one in both:
+            getattr(one, step)()
+
+
+def reduce_all(first_grad, second_grad, scale):
+    def prepared(grad):
+        flat = grad.reshape(ROWS, 128).astype(jnp.bfloat16)
+        return jnp.pad(flat, ((0, FULL - ROWS), (0, 0)))
+
+    shape = jax.ShapeDtypeStruct((FULL, 128), jnp.bfloat16)
+    first, second = pl.pallas_call(
+        functools.partial(reduce_kernel, scale),
+        out_shape=(shape, shape),
+        in_specs=[pl.BlockSpec(memory_space=pltpu.VMEM)] * 2,
+        out_specs=[pl.BlockSpec(memory_space=pltpu.VMEM)] * 2,
+        scratch_shapes=Reduce.scratch * 2,
+        compiler_params=pltpu.CompilerParams(
+            collective_id=0, has_side_effects=True, vmem_limit_bytes=32 * 1024 * 1024
+        ),
+        cost_estimate=pl.CostEstimate(
+            flops=FULL * 128 * 4, bytes_accessed=8 * FULL * 128, transcendentals=0
+        ),
+    )(prepared(first_grad), prepared(second_grad))
+    return first[:ROWS].reshape(27, 128, 128), second[:ROWS].reshape(27, 128, 128)
 
 
 def padded(block, sides, width):
@@ -112,7 +437,6 @@
     grads_x, first_grad = transpose_conv(
         first_delta, picked_x, in_rows, out_rows, live_rows, first_weight, table_rows
     )
-    first_grad, second_grad = lax.psum((first_grad, second_grad), ("gx", "gy"))
     input_grad = return_rim(grads_x, blocks) + second_delta.astype(jnp.float32)
     scale = 1.0 / math.sqrt(
         lax.axis_size("gx")
@@ -121,11 +445,12 @@
         * in_rows.shape[1]
         * shape_tail[0]
     )
+    first_grad, second_grad = reduce_all(first_grad, second_grad, scale)
     return (
         result.reshape(voxels.shape),
         input_grad.astype(jnp.bfloat16).reshape(voxels.shape),
-        (first_grad * scale).astype(jnp.bfloat16),
-        (second_grad * scale).astype(jnp.bfloat16),
+        first_grad,
+        second_grad,
     )
 
 

time: 621 us -> 196 us (0.32)
  waiting for transfers between devices: 491 us -> 28.1 us
  Pallas kernels: 0 us -> 63.8 us
  between operations: 14.8 us -> 1.46 us
  starting transfers between devices: 56.6 us -> 45.1 us
    psum x1 -> x0, waiting for transfers between devices: 481 us -> none  [shards(): first_grad, second_grad = lax.psum((first_grad, second_grad), ('gx', 'gy'))]
    pallas_call x0 -> x1, Pallas kernels: none -> 63.8 us  [reduce_all(): pl.pallas_call(functools.partial(reduce_kernel, scale), out_shape=(shape,...]
    ppermute x8, waiting for transfers between devices: 1.88 us -> 27 us  [padded(): lax.ppermute(lax.slice_in_dim(block, 0, width, axis=dim), axis, backward)]
    ppermute x8, waiting for transfers between devices: 8.4 us -> 1.15 us  [padded(): lax.ppermute(lax.slice_in_dim(block, block.shape[dim] - width, None, axis...]
    ppermute x8, starting transfers between devices: 21.4 us -> 15 us  [padded(): lax.ppermute(lax.slice_in_dim(block, 0, width, axis=dim), axis, backward)]
  transfers between devices with their start and end apart: 17 -> 16, of which waited for: 10 -> 8; matrix products, arithmetic and copies ran while one was open for 2% -> 6% of each run, Pallas kernels for 0% -> 33%
where the time goes in v1:
time: 196 us; the launch traced here: 195 us
  Pallas kernels  63.8 us (33%)
  starting transfers between devices  45.1 us (23%)
  local copies, waits for them, and re-layouts  33.6 us (17%)
  waiting for transfers between devices  28.1 us (14%)
  matrix products  15.6 us (8%)
  other arithmetic  7.02 us (4%)
    pallas_call x1, Pallas kernels, reduce_all(): pl.pallas_call(functools.partial(reduce_kernel, scale), out_shape=(shape,...  63.8 us
    ppermute x8, starting transfers between devices, padded(): lax.ppermute(lax.slice_in_dim(block, block.shape[dim] - width, None, axis...  30.1 us
    ppermute x8, waiting for transfers between devices, padded(): lax.ppermute(lax.slice_in_dim(block, 0, width, axis=dim), axis, backward)  27 us
    ppermute x8, starting transfers between devices, padded(): lax.ppermute(lax.slice_in_dim(block, 0, width, axis=dim), axis, backward)  15 us
    unnamed x59, local copies, waits for them, and re-layouts  12.2 us
    reshape x2, local copies, waits for them, and re-layouts, transpose_conv(): backward = backward.reshape(offsets * slot_count, voxel_count * width)  5.39 us
    dot_general x2, matrix products, transpose_conv(): jnp.dot(placing, backward, precision=lax.Precision.HIGHEST, preferred_ele...  4.46 us
    reshape x2, local copies, waits for them, and re-layouts, convolve(): product = product.reshape(offsets * slot_count, voxel_count * width)  4.28 us
  transfers between devices with their start and end apart: 16, of which 8 were waited for; matrix products, arithmetic and copies ran while one was open for 6% of the time, Pallas kernels for 33%

profile of v1, /device:TPU:1, one launch (start us, length us, event | category | flops | bytes accessed | tf_op | source)
XLA Modules:
  0.0 194.7 jit_solution(8886246728621073805)
XLA Ops:
  1.5 6.0 %collective-permute-start = (bf16[1,1,2,64,128]{4,3,2,1,0:T(8,128)(2,1)S(1)}, bf16[1,1,2,64,128]{4,3,2,1,0:T(8,128)(2,1)S(1)}, u32[]{:S(2)}, u32[]{:S(2)}) collective-permute-start(bf16[1,1,2,64,128]{4,3,2,1,0:T(8,128)(2,1)S(1)} %slice.183), channel_id=1, source_target_pairs={{0,8},{8,16},{16,24},{24,32},{32,40},{40,48},{48,56},{56,64},{64,7... | collective-permute-start | bytes 98312 | tf_op jit(solution)/shard_map/ppermute | solution.py:341
  7.5 4.0 %collective-permute-start.1 = (bf16[1,1,2,64,128]{4,3,2,1,0:T(8,128)(2,1)S(1)}, bf16[1,1,2,64,128]{4,3,2,1,0:T(8,128)(2,1)S(1)}, u32[]{:S(2)}, u32[]{:S(2)}) collective-permute-start(bf16[1,1,2,64,128]{4,3,2,1,0:T(8,128)(2,1)S(1)} %slice.183), channel_id=1, source_target_pairs={{8,0},{16,8},{24,16},{32,24},{40,32},{48,40},{56,48},{64,56},{72,6... | collective-permute-start | bytes 98312 | tf_op jit(solution)/shard_map/ppermute | solution.py:344
  19.8 4.2 %collective-permute-done.3 = bf16[3,1,2,64,128]{4,3,2,1,0:T(8,128)(2,1)S(1)} collective-permute-done((bf16[3,1,2,64,128]{4,3,2,1,0:T(8,128)(2,1)S(1)}, bf16[3,1,2,64,128]{4,3,2,1,0:T(8,128)(2,1)S(1)}, u32[]{:S(2)}, u32[]{:S(2)}) %collective-permute-start.3) | collective-permute-done | bytes 98336 | tf_op jit(solution)/shard_map/ppermute | solution.py:344
  26.8 1.6 reshape.214
  28.4 1.8 copy.59
  30.5 2.4 %multiply_convert_fusion.2 = (bf16[8,64,128]{2,0,1:T(8,128)(2,1)S(1)}, f32[8,64,128]{2,0,1:T(8,128)}) fusion(f32[64,128,54]{1,0,2:T(8,128)S(1)} %slice_bitcast_fusion.1, s32[54]{0:T(128)S(1)} %eq.10, pred[54]{0:T(512)(128)(4,1)S(1)} %gt.13), kind=kOutput, calls=%fused_computation.37 | convolution fusion | flops 42795872 | bytes 2162958 | tf_op jit(solution)/shard_map/dot_general | solution.py:391
  32.9 5.3 %collective-permute-start.4 = (bf16[1,1,2,64,128]{4,2,3,1,0:T(2,128)(2,1)S(1)}, bf16[1,1,2,64,128]{4,2,3,1,0:T(2,128)(2,1)S(1)}, u32[]{:S(2)}, u32[]{:S(2)}) collective-permute-start(bf16[1,1,2,64,128]{4,2,3,1,0:T(2,128)(2,1)S(1)} %slice_bitcast_fusion.14), channel_id=1, source_target_pairs={{0,8},{8,16},{16,24},{24,32},{32,40},{40,48},{48,56},{56,64},{64,7... | collective-permute-start | bytes 98312 | tf_op jit(solution)/shard_map/ppermute | solution.py:341
  38.2 1.9 collective-permute-start.5
  41.7 3.2 %collective-permute-done.5 = bf16[1,1,2,64,128]{4,2,3,1,0:T(2,128)(2,1)S(1)} collective-permute-done((bf16[1,1,2,64,128]{4,2,3,1,0:T(2,128)(2,1)S(1)}, bf16[1,1,2,64,128]{4,2,3,1,0:T(2,128)(2,1)S(1)}, u32[]{:S(2)}, u32[]{:S(2)}) %collective-permute-start.5) | collective-permute-done | bytes 32800 | tf_op jit(solution)/shard_map/ppermute | solution.py:344
  45.1 3.2 %collective-permute-start.6 = (bf16[3,1,2,64,128]{4,2,3,1,0:T(2,128)(2,1)S(1)}, bf16[3,1,2,64,128]{4,2,3,1,0:T(2,128)(2,1)S(1)}, u32[]{:S(2)}, u32[]{:S(2)}) collective-permute-start(bf16[3,1,2,64,128]{4,2,3,1,0:T(2,128)(2,1)S(1)} %pad_maximum_fusion.9), channel_id=1, source_target_pairs={{0,1},{1,2},{2,3},{3,4},{4,5},{5,6},{6,7},{8,9},{9,10},{10,11},{11... | collective-permute-start | bytes 294920 | tf_op jit(solution)/shard_map/ppermute | solution.py:341
  50.0 3.7 %collective-permute-done.7 = bf16[3,1,2,64,128]{4,2,3,1,0:T(2,128)(2,1)S(1)} collective-permute-done((bf16[3,1,2,64,128]{4,2,3,1,0:T(2,128)(2,1)S(1)}, bf16[3,1,2,64,128]{4,2,3,1,0:T(2,128)(2,1)S(1)}, u32[]{:S(2)}, u32[]{:S(2)}) %collective-permute-start.7) | collective-permute-done | bytes 98336 | tf_op jit(solution)/shard_map/ppermute | solution.py:344
  56.3 1.6 fusion.43
  57.9 2.7 %reshape.219 = f32[54,8192]{1,0:T(8,128)} reshape(f32[27,128,128]{2,1,0:T(8,128)} %fusion.43) | data formatting | bytes 3538944 | tf_op jit(solution)/shard_map/reshape | solution.py:386
  60.6 1.8 copy.60
  63.4 1.8 fusion.7
  65.3 1.6 gather_fusion.2
  69.2 2.0 %fusion.44 = f32[27,128,128]{2,1,0:T(8,128)} fusion(bf16[27,128,128]{2,1,0:T(8,128)(2,1)S(1)} %bitcast.137, bf16[27,128,128]{2,1,0:T(8,128)(2,1)S(1)} %copy-done), kind=kOutput, calls=%fused_computation.90 | convolution fusion | flops 113246208 | bytes 3538944 | tf_op jit(solution)/shard_map/kmd,kcd->kmc/dot_general | solution.py:404
  71.2 2.7 %reshape.222 = f32[54,8192]{1,0:T(8,128)} reshape(f32[27,128,128]{2,1,0:T(8,128)} %fusion.44) | data formatting | bytes 3538944 | tf_op jit(solution)/shard_map/reshape | solution.py:405
  73.9 2.2 %fusion.23 = f32[24,8192]{1,0:T(8,128)S(1)} fusion(f32[54,8192]{1,0:T(8,128)} %reshape.222, s32[54]{0:T(128)S(1)} %reshape_reshape.2), kind=kOutput, calls=%fused_computation.67 | convolution fusion | flops 127403280 | bytes 2556120 | tf_op jit(solution)/shard_map/dot_general | solution.py:408
  76.4 3.5 %collective-permute-start.8 = (f32[1,3,2,64,128]{4,2,3,1,0:T(2,128)S(1)}, f32[1,3,2,64,128]{4,2,3,1,0:T(2,128)S(1)}, u32[]{:S(2)}, u32[]{:S(2)}) collective-permute-start(f32[1,3,2,64,128]{4,2,3,1,0:T(2,128)S(1)} %copy.40), channel_id=1, source_target_pairs={{0,8},{8,16},{16,24},{24,32},{32,40},{40,48},{48,56},{56,64},{64,7... | collective-permute-start | bytes 589832 | tf_op jit(solution)/shard_map/ppermute | solution.py:341
  80.1 1.9 collective-permute-start.9
  82.7 5.9 %collective-permute-done.9 = f32[1,3,2,64,128]{4,2,3,1,0:T(2,128)S(1)} collective-permute-done((f32[1,3,2,64,128]{4,2,3,1,0:T(2,128)S(1)}, f32[1,3,2,64,128]{4,2,3,1,0:T(2,128)S(1)}, u32[]{:S(2)}, u32[]{:S(2)}) %collective-permute-start.9) | collective-permute-done | bytes 196640 | tf_op jit(solution)/shard_map/ppermute | solution.py:344
  88.8 4.3 %collective-permute-start.10 = (f32[1,2,64,128]{3,1,2,0:T(2,128)S(1)}, f32[1,2,64,128]{3,1,2,0:T(2,128)S(1)}, u32[]{:S(2)}, u32[]{:S(2)}) collective-permute-start(f32[1,2,64,128]{3,1,2,0:T(2,128)S(1)} %get-tuple-element.60), channel_id=1, source_target_pairs={{0,1},{1,2},{2,3},{3,4},{4,5},{5,6},{6,7},{8,9},{9,10},{10,11},{11... | collective-permute-start | bytes 196616 | tf_op jit(solution)/shard_map/ppermute | solution.py:341
  95.7 2.7 %collective-permute-done.11 = f32[1,2,64,128]{3,1,2,0:T(2,128)S(1)} collective-permute-done((f32[1,2,64,128]{3,1,2,0:T(2,128)S(1)}, f32[1,2,64,128]{3,1,2,0:T(2,128)S(1)}, u32[]{:S(2)}, u32[]{:S(2)}) %collective-permute-start.11) | collective-permute-done | bytes 65568 | tf_op jit(solution)/shard_map/ppermute | solution.py:344
  102.6 2.0 %fusion.45 = f32[27,128,128]{2,1,0:T(8,128)} fusion(bf16[27,128,128]{2,1,0:T(8,128)(2,1)S(1)} %bitcast.135, bf16[27,128,128]{2,1,0:T(8,128)(2,1)S(1)} %copy-done.6), kind=kOutput, calls=%fused_computation.91 | convolution fusion | flops 113246208 | bytes 3538944 | tf_op jit(solution)/shard_map/kmd,kcd->kmc/dot_general | solution.py:404
  104.5 2.7 %reshape.225 = f32[54,8192]{1,0:T(8,128)} reshape(f32[27,128,128]{2,1,0:T(8,128)} %fusion.45) | data formatting | bytes 3538944 | tf_op jit(solution)/shard_map/reshape | solution.py:405
  107.2 2.2 %fusion.22 = f32[24,8192]{1,0:T(8,128)S(1)} fusion(f32[54,8192]{1,0:T(8,128)} %reshape.225, s32[54]{0:T(128)S(1)} %reshape_reshape.2), kind=kOutput, calls=%fused_computation.66 | convolution fusion | flops 127403280 | bytes 2556120 | tf_op jit(solution)/shard_map/dot_general | solution.py:408
  109.7 2.9 %collective-permute-start.12 = (f32[1,3,2,64,128]{4,2,3,1,0:T(2,128)S(1)}, f32[1,3,2,64,128]{4,2,3,1,0:T(2,128)S(1)}, u32[]{:S(2)}, u32[]{:S(2)}) collective-permute-start(f32[1,3,2,64,128]{4,2,3,1,0:T(2,128)S(1)} %copy.45), channel_id=1, source_target_pairs={{0,8},{8,16},{16,24},{24,32},{32,40},{40,48},{48,56},{56,64},{64,7... | collective-permute-start | bytes 589832 | tf_op jit(solution)/shard_map/ppermute | solution.py:341
  112.8 1.9 collective-permute-start.13
  115.4 7.1 %collective-permute-done.13 = f32[1,3,2,64,128]{4,2,3,1,0:T(2,128)S(1)} collective-permute-done((f32[1,3,2,64,128]{4,2,3,1,0:T(2,128)S(1)}, f32[1,3,2,64,128]{4,2,3,1,0:T(2,128)S(1)}, u32[]{:S(2)}, u32[]{:S(2)}) %collective-permute-start.13) | collective-permute-done | bytes 196640 | tf_op jit(solution)/shard_map/ppermute | solution.py:344
  122.7 3.5 %collective-permute-start.14 = (f32[1,2,64,128]{3,1,2,0:T(2,128)S(1)}, f32[1,2,64,128]{3,1,2,0:T(2,128)S(1)}, u32[]{:S(2)}, u32[]{:S(2)}) collective-permute-start(f32[1,2,64,128]{3,1,2,0:T(2,128)S(1)} %get-tuple-element.58), channel_id=1, source_target_pairs={{0,1},{1,2},{2,3},{3,4},{4,5},{5,6},{6,7},{8,9},{9,10},{10,11},{11... | collective-permute-start | bytes 196616 | tf_op jit(solution)/shard_map/ppermute | solution.py:341
  128.1 63.8 %shard_map.102 = (bf16[3584,128]{1,0:T(8,128)(2,1)S(1)}, bf16[3584,128]{1,0:T(8,128)(2,1)S(1)}) custom-call(bf16[3584,128]{1,0:T(8,128)(2,1)S(1)} %pad.11.first_part, bf16[3584,128]{1,0:T(8,128)(2,1)S(1)} %pad.12.second_part), custom_call_target="tpu_custom_call" | custom-call | flops 1835008 | bytes 3670016 | tf_op jit(solution)/shard_map/pallas_call | solution.py:320
  (132 shorter events, 34.7 us)
Async XLA Ops:
  0.6 55.7 %copy-start = (bf16[27,128,128]{2,1,0:T(8,128)(2,1)S(1)}, bf16[27,128,128]{2,1,0:T(8,128)(2,1)}, u32[]{:S(2)}) copy-start(bf16[27,128,128]{2,1,0:T(8,128)(2,1)} %param.17) | copy-start | bytes 2654212
  1.5 14.8 %collective-permute-start = (bf16[1,1,2,64,128]{4,3,2,1,0:T(8,128)(2,1)S(1)}, bf16[1,1,2,64,128]{4,3,2,1,0:T(8,128)(2,1)S(1)}, u32[]{:S(2)}, u32[]{:S(2)}) collective-permute-start(bf16[1,1,2,64,128]{4,3,2,1,0:T(8,128)(2,1)S(1)} %slice.183), channel_id=1, source_target_pairs={{0,8},{8,16},{16,24},{24,32},{32,40},{40,48},{48,56},{56,64},{64,7... | collective-permute-start | bytes 98312 | tf_op jit(solution)/shard_map/ppermute | solution.py:341
  7.5 8.8 %collective-permute-start.1 = (bf16[1,1,2,64,128]{4,3,2,1,0:T(8,128)(2,1)S(1)}, bf16[1,1,2,64,128]{4,3,2,1,0:T(8,128)(2,1)S(1)}, u32[]{:S(2)}, u32[]{:S(2)}) collective-permute-start(bf16[1,1,2,64,128]{4,3,2,1,0:T(8,128)(2,1)S(1)} %slice.183), channel_id=1, source_target_pairs={{8,0},{16,8},{24,16},{32,24},{40,32},{48,40},{56,48},{64,56},{72,6... | collective-permute-start | bytes 98312 | tf_op jit(solution)/shard_map/ppermute | solution.py:344
  14.4 10.9 %copy-start.14 = (pred[54]{0:T(512)(128)(4,1)}, pred[54]{0:T(512)(128)(4,1)S(1)}, u32[]{:S(2)}) copy-start(pred[54]{0:T(512)(128)(4,1)S(1)} %get-tuple-element.67) | copy-start | bytes 166
  16.3 14.2 %copy-start.12 = (pred[54]{0:T(512)(128)(4,1)}, pred[54]{0:T(512)(128)(4,1)S(1)}, u32[]{:S(2)}) copy-start(pred[54]{0:T(512)(128)(4,1)S(1)} %gt.13) | copy-start | bytes 166
  16.3 3.5 %collective-permute-start.2 = (bf16[3,1,2,64,128]{4,3,2,1,0:T(8,128)(2,1)S(1)}, bf16[3,1,2,64,128]{4,3,2,1,0:T(8,128)(2,1)S(1)}, u32[]{:S(2)}, u32[]{:S(2)}) collective-permute-start(bf16[3,1,2,64,128]{4,3,2,1,0:T(8,128)(2,1)S(1)} %pad_maximum_fusion.8), channel_id=1, source_target_pairs={{0,1},{1,2},{2,3},{3,4},{4,5},{5,6},{6,7},{8,9},{9,10},{10,11},{11... | collective-permute-start | bytes 294920 | tf_op jit(solution)/shard_map/ppermute | solution.py:341
  17.6 6.4 %collective-permute-start.3 = (bf16[3,1,2,64,128]{4,3,2,1,0:T(8,128)(2,1)S(1)}, bf16[3,1,2,64,128]{4,3,2,1,0:T(8,128)(2,1)S(1)}, u32[]{:S(2)}, u32[]{:S(2)}) collective-permute-start(bf16[3,1,2,64,128]{4,3,2,1,0:T(8,128)(2,1)S(1)} %pad_maximum_fusion.8), channel_id=1, source_target_pairs={{1,0},{2,1},{3,2},{4,3},{5,4},{6,5},{7,6},{9,8},{10,9},{11,10},{12... | collective-permute-start | bytes 294920 | tf_op jit(solution)/shard_map/ppermute | solution.py:344
  25.3 1.2 copy-start.5
  30.4 9.7 %copy-start.17 = (s32[1,1,27,2]{2,3,1,0:T(2,128)S(1)}, s32[1,1,27,2]{2,3,1,0:T(2,128)}, u32[]{:S(2)}) copy-start(s32[1,1,27,2]{2,3,1,0:T(2,128)} %param.20) | copy-start | bytes 652
  30.5 19.2 %copy-start.16 = (s32[54]{0:T(128)S(1)}, s32[54]{0:T(128)}, u32[]{:S(2)}) copy-start(s32[54]{0:T(128)} %get-tuple-element.64) | copy-start | bytes 652
  32.9 8.8 %collective-permute-start.4 = (bf16[1,1,2,64,128]{4,2,3,1,0:T(2,128)(2,1)S(1)}, bf16[1,1,2,64,128]{4,2,3,1,0:T(2,128)(2,1)S(1)}, u32[]{:S(2)}, u32[]{:S(2)}) collective-permute-start(bf16[1,1,2,64,128]{4,2,3,1,0:T(2,128)(2,1)S(1)} %slice_bitcast_fusion.14), channel_id=1, source_target_pairs={{0,8},{8,16},{16,24},{24,32},{32,40},{40,48},{48,56},{56,64},{64,7... | collective-permute-start | bytes 98312 | tf_op jit(solution)/shard_map/ppermute | solution.py:341
  38.2 6.7 %collective-permute-start.5 = (bf16[1,1,2,64,128]{4,2,3,1,0:T(2,128)(2,1)S(1)}, bf16[1,1,2,64,128]{4,2,3,1,0:T(2,128)(2,1)S(1)}, u32[]{:S(2)}, u32[]{:S(2)}) collective-permute-start(bf16[1,1,2,64,128]{4,2,3,1,0:T(2,128)(2,1)S(1)} %slice_bitcast_fusion.14), channel_id=1, source_target_pairs={{8,0},{16,8},{24,16},{32,24},{40,32},{48,40},{56,48},{64,56},{72,6... | collective-permute-start | bytes 98312 | tf_op jit(solution)/shard_map/ppermute | solution.py:344
  45.1 4.8 %collective-permute-start.6 = (bf16[3,1,2,64,128]{4,2,3,1,0:T(2,128)(2,1)S(1)}, bf16[3,1,2,64,128]{4,2,3,1,0:T(2,128)(2,1)S(1)}, u32[]{:S(2)}, u32[]{:S(2)}) collective-permute-start(bf16[3,1,2,64,128]{4,2,3,1,0:T(2,128)(2,1)S(1)} %pad_maximum_fusion.9), channel_id=1, source_target_pairs={{0,1},{1,2},{2,3},{3,4},{4,5},{5,6},{6,7},{8,9},{9,10},{10,11},{11... | collective-permute-start | bytes 294920 | tf_op jit(solution)/shard_map/ppermute | solution.py:341
  48.3 5.4 %collective-permute-start.7 = (bf16[3,1,2,64,128]{4,2,3,1,0:T(2,128)(2,1)S(1)}, bf16[3,1,2,64,128]{4,2,3,1,0:T(2,128)(2,1)S(1)}, u32[]{:S(2)}, u32[]{:S(2)}) collective-permute-start(bf16[3,1,2,64,128]{4,2,3,1,0:T(2,128)(2,1)S(1)} %pad_maximum_fusion.9), channel_id=1, source_target_pairs={{1,0},{2,1},{3,2},{4,3},{5,4},{6,5},{7,6},{9,8},{10,9},{11,10},{12... | collective-permute-start | bytes 294920 | tf_op jit(solution)/shard_map/ppermute | solution.py:344
  62.5 1.0 copy-start.9
  62.5 1.0 copy-start.13
  63.4 3.5 %copy-start.10 = (bf16[54]{0:T(256)(128)(2,1)S(1)}, bf16[54]{0:T(256)(128)(2,1)}, u32[]{:S(2)}) copy-start(bf16[54]{0:T(256)(128)(2,1)} %convert_element_type.65) | copy-start | bytes 328
  63.4 3.5 %copy-start.11 = (pred[54]{0:T(512)(128)(4,1)S(1)}, pred[54]{0:T(512)(128)(4,1)}, u32[]{:S(2)}) copy-start(pred[54]{0:T(512)(128)(4,1)} %get-tuple-element.66) | copy-start | bytes 166
  76.4 6.3 %collective-permute-start.8 = (f32[1,3,2,64,128]{4,2,3,1,0:T(2,128)S(1)}, f32[1,3,2,64,128]{4,2,3,1,0:T(2,128)S(1)}, u32[]{:S(2)}, u32[]{:S(2)}) collective-permute-start(f32[1,3,2,64,128]{4,2,3,1,0:T(2,128)S(1)} %copy.40), channel_id=1, source_target_pairs={{0,8},{8,16},{16,24},{24,32},{32,40},{40,48},{48,56},{56,64},{64,7... | collective-permute-start | bytes 589832 | tf_op jit(solution)/shard_map/ppermute | solution.py:341
  80.1 8.5 %copy-start.15 = (f32[3]{0:T(128)S(1)}, f32[3]{0:T(128)}, u32[]{:S(2)}) copy-start(f32[3]{0:T(128)} %slice.239) | copy-start | bytes 40
  80.1 8.5 %collective-permute-start.9 = (f32[1,3,2,64,128]{4,2,3,1,0:T(2,128)S(1)}, f32[1,3,2,64,128]{4,2,3,1,0:T(2,128)S(1)}, u32[]{:S(2)}, u32[]{:S(2)}) collective-permute-start(f32[1,3,2,64,128]{4,2,3,1,0:T(2,128)S(1)} %copy.43), channel_id=1, source_target_pairs={{8,0},{16,8},{24,16},{32,24},{40,32},{48,40},{56,48},{64,56},{72,6... | collective-permute-start | bytes 589832 | tf_op jit(solution)/shard_map/ppermute | solution.py:344
  82.1 12.3 %copy-start.4 = (bf16[54,64,128]{2,1,0:T(8,128)(2,1)S(1)}, bf16[54,64,128]{2,1,0:T(8,128)(2,1)}, u32[]{:S(2)}) copy-start(bf16[54,64,128]{2,1,0:T(8,128)(2,1)} %copy-done.3) | copy-start | bytes 2654212
  88.8 6.8 %collective-permute-start.10 = (f32[1,2,64,128]{3,1,2,0:T(2,128)S(1)}, f32[1,2,64,128]{3,1,2,0:T(2,128)S(1)}, u32[]{:S(2)}, u32[]{:S(2)}) collective-permute-start(f32[1,2,64,128]{3,1,2,0:T(2,128)S(1)} %get-tuple-element.60), channel_id=1, source_target_pairs={{0,1},{1,2},{2,3},{3,4},{4,5},{5,6},{6,7},{8,9},{9,10},{10,11},{11... | collective-permute-start | bytes 196616 | tf_op jit(solution)/shard_map/ppermute | solution.py:341
  93.1 5.3 %collective-permute-start.11 = (f32[1,2,64,128]{3,1,2,0:T(2,128)S(1)}, f32[1,2,64,128]{3,1,2,0:T(2,128)S(1)}, u32[]{:S(2)}, u32[]{:S(2)}) collective-permute-start(f32[1,2,64,128]{3,1,2,0:T(2,128)S(1)} %get-tuple-element.61), channel_id=1, source_target_pairs={{1,0},{2,1},{3,2},{4,3},{5,4},{6,5},{7,6},{9,8},{10,9},{11,10},{12... | collective-permute-start | bytes 196616 | tf_op jit(solution)/shard_map/ppermute | solution.py:344
  94.9 3.6 %copy-start.7 = (f32[8,64,128]{2,0,1:T(8,128)S(1)}, f32[8,64,128]{2,0,1:T(8,128)}, u32[]{:S(2)}) copy-start(f32[8,64,128]{2,0,1:T(8,128)} %get-tuple-element.63) | copy-start | bytes 786436
  100.2 2.4 %copy-start.6 = (bf16[27,128,128]{2,1,0:T(8,128)(2,1)S(1)}, bf16[27,128,128]{2,1,0:T(8,128)(2,1)}, u32[]{:S(2)}) copy-start(bf16[27,128,128]{2,1,0:T(8,128)(2,1)} %param.16) | copy-start | bytes 2654212
  101.7 0.9 copy-start.1
  109.7 5.7 %collective-permute-start.12 = (f32[1,3,2,64,128]{4,2,3,1,0:T(2,128)S(1)}, f32[1,3,2,64,128]{4,2,3,1,0:T(2,128)S(1)}, u32[]{:S(2)}, u32[]{:S(2)}) collective-permute-start(f32[1,3,2,64,128]{4,2,3,1,0:T(2,128)S(1)} %copy.45), channel_id=1, source_target_pairs={{0,8},{8,16},{16,24},{24,32},{32,40},{40,48},{48,56},{56,64},{64,7... | collective-permute-start | bytes 589832 | tf_op jit(solution)/shard_map/ppermute | solution.py:341
  112.8 9.6 %collective-permute-start.13 = (f32[1,3,2,64,128]{4,2,3,1,0:T(2,128)S(1)}, f32[1,3,2,64,128]{4,2,3,1,0:T(2,128)S(1)}, u32[]{:S(2)}, u32[]{:S(2)}) collective-permute-start(f32[1,3,2,64,128]{4,2,3,1,0:T(2,128)S(1)} %copy.48), channel_id=1, source_target_pairs={{8,0},{16,8},{24,16},{32,24},{40,32},{48,40},{56,48},{64,56},{72,6... | collective-permute-start | bytes 589832 | tf_op jit(solution)/shard_map/ppermute | solution.py:344
  114.8 12.7 %copy-start.2 = (bf16[54,64,128]{2,1,0:T(8,128)(2,1)S(1)}, bf16[54,64,128]{2,1,0:T(8,128)(2,1)}, u32[]{:S(2)}) copy-start(bf16[54,64,128]{2,1,0:T(8,128)(2,1)} %copy-done.1) | copy-start | bytes 2654212
  122.7 71.2 %collective-permute-start.14 = (f32[1,2,64,128]{3,1,2,0:T(2,128)S(1)}, f32[1,2,64,128]{3,1,2,0:T(2,128)S(1)}, u32[]{:S(2)}, u32[]{:S(2)}) collective-permute-start(f32[1,2,64,128]{3,1,2,0:T(2,128)S(1)} %get-tuple-element.58), channel_id=1, source_target_pairs={{0,1},{1,2},{2,3},{3,4},{4,5},{5,6},{6,7},{8,9},{9,10},{10,11},{11... | collective-permute-start | bytes 196616 | tf_op jit(solution)/shard_map/ppermute | solution.py:341
  126.3 67.6 %collective-permute-start.15 = (f32[1,2,64,128]{3,1,2,0:T(2,128)S(1)}, f32[1,2,64,128]{3,1,2,0:T(2,128)S(1)}, u32[]{:S(2)}, u32[]{:S(2)}) collective-permute-start(f32[1,2,64,128]{3,1,2,0:T(2,128)S(1)} %get-tuple-element.59), channel_id=1, source_target_pairs={{1,0},{2,1},{3,2},{4,3},{5,4},{6,5},{7,6},{9,8},{10,9},{11,10},{12... | collective-permute-start | bytes 196616 | tf_op jit(solution)/shard_map/ppermute | solution.py:344
  (2 other events, 1.8 us)

commit v2 on v1

--- a/solution.py
+++ b/solution.py
@@ -289,168 +289,352 @@
     pl.semaphore_wait(barrier, len(peers) + 15)
 
 
-def reduce_kernel(scale, first_part, second_part, first_out, second_out, *scratch):
-    enter(group_peers())
+BLOCKS, VOXELS, OFFSETS, SLOTS, TABLE = 8, 64, 27, 54, 24
+DIRECTIONS = [(a, b) for a in (-1, 0, 1) for b in (-1, 0, 1) if (a, b) != (0, 0)]
+
+
+def neighbour(direction):
+    a, b = direction
+    gx, gy = lax.axis_index("gx"), lax.axis_index("gy")
+    return lax.rem(gx + a + 64, 64), lax.rem(gy + b + 8, 8)
+
+
+def present(direction):
+    a, b = direction
+    gx, gy = lax.axis_index("gx") + a, lax.axis_index("gy") + b
+    return (gx >= 0) & (gx < 64) & (gy >= 0) & (gy < 8)
+
+
+def sigmoid(values):
+    return 1.0 / (1.0 + jnp.exp(-values))
+
+
+def slope(values):
+    s = sigmoid(values)
+    return s * (1.0 + values * (1.0 - s))
+
+
+def write_plan(in_ref, out_ref, live_ref, plan):
+    shape = (OFFSETS, 128)
+    lane = lax.broadcasted_iota(jnp.int32, shape, 1)
+    even = 2 * lax.broadcasted_iota(jnp.int32, shape, 0)
+
+    def columns(values):
+        return [jnp.broadcast_to(values[:, s : s + 1], shape) for s in (0, 1)]
+
+    def along(pair):
+        picked = jnp.where(lane == even, pair[0], 0) + jnp.where(lane == even + 1, pair[1], 0)
+        return jnp.sum(picked, axis=0, keepdims=True)
+
+    def chain(pair):
+        target = jnp.broadcast_to(along(pair), shape)
+        found = jnp.zeros(shape, jnp.int32)
+        last = jnp.zeros(shape, jnp.int32)
+        for s in (0, 1):
+            same = (pair[s] == target) & (even + s < lane) & (pair[s] >= 0)
+            found = jnp.maximum(found, jnp.where(same, even + s + 1, 0))
+            last = jnp.maximum(last, jnp.where(pair[s] == lane, even + s + 1, 0))
+        return jnp.max(found, axis=0, keepdims=True), jnp.max(last, axis=0, keepdims=True)
+
+    source, target, live = in_ref[...], out_ref[...], live_ref[...]
+    plan[0:1] = along(columns(source))
+    plan[1:2] = along(columns(jnp.where(live > 0, target, BLOCKS)))
+    plan[2:3], plan[3:4] = chain(columns(jnp.where(live > 0, target, -1)))
+    plan[4:5], plan[5:6] = chain(columns(jnp.where(live > 0, source, -1)))
+    plan[6:8] = jnp.zeros((2, 128), jnp.int32)
+
+
+def step_loop(body):
+    @pl.loop(0, OFFSETS // 3)
+    def _(step):
+        for u in range(3):
+            body(step * 3 + u)
+
+
+def pair_of(table, plan, row, k):
+    return jnp.concatenate([table[plan[row, 2 * k]], table[plan[row, 2 * k + 1]]], axis=0)
+
+
+def convolve(table, plan, row, chain, weight, sums, flipped):
+    def body(k):
+        product = lax.dot_general(
+            pair_of(table, plan, row, k),
+            weight[k],
+            (((1,), (1 if flipped else 0,)), ((), ())),
+            preferred_element_type=jnp.float32,
+        )
+        sums[2 * k + 1] = sums[plan[chain, 2 * k]] + product[:VOXELS]
+        sums[2 * k + 2] = sums[plan[chain, 2 * k + 1]] + product[VOXELS:]
+
+    step_loop(body)
+
+
+def weight_terms(table, delta, plan, part):
+    def body(k):
+        product = lax.dot_general(
+            pair_of(table, plan, 0, k),
+            pair_of(delta, plan, 1, k),
+            (((0,), (0,)), ((), ())),
+            preferred_element_type=jnp.float32,
+        )
+        part[rows(k * 128, 128)] = product.astype(jnp.bfloat16)
+
+    step_loop(body)
+
+
+class Swap:
+    def __init__(self, index, send_sems, recv_sems, sources, targets):
+        self.copies = []
+        for g, direction in enumerate(DIRECTIONS):
+            copy = pltpu.make_async_remote_copy(
+                src_ref=sources[g],
+                dst_ref=targets[7 - g],
+                send_sem=send_sems.at[index, g],
+                recv_sem=recv_sems.at[index, 7 - g],
+                device_id=neighbour(direction),
+                device_id_type=MESH,
+            )
+            copy.start()
+            self.copies.append(copy)
+
+    def arrive(self):
+        for copy in self.copies:
+            copy.wait_recv()
+
+    def finish(self):
+        for copy in self.copies:
+            copy.wait_send()
+
+
+def rim_slots(table):
+    return [table.at[pl.ds(BLOCKS + RIM * g, RIM)] for g in range(8)]
+
+
+def clear_outside(table):
+    for g, direction in enumerate(DIRECTIONS):
+
+        @pl.when(jnp.logical_not(present(direction)))
+        def _():
+            table[BLOCKS + RIM * g : BLOCKS + RIM * (g + 1)] = jnp.zeros(
+                (RIM, VOXELS, 128), jnp.bfloat16
+            )
+
+
+def routed(own, arrived, r):
+    total = own
+    for g, direction in enumerate(DIRECTIONS):
+        total = total + jnp.where(present(direction), arrived[g, r].astype(jnp.float32), 0.0)
+    return total
+
+
+BLOCK_SET = (VOXELS, 128)
+SCRATCH = [
+    pltpu.VMEM((8, 128), jnp.int32),
+    pltpu.SMEM((8, 128), jnp.int32),
+    pltpu.VMEM((TABLE,) + BLOCK_SET, jnp.bfloat16),
+    pltpu.VMEM((TABLE,) + BLOCK_SET, jnp.bfloat16),
+    pltpu.VMEM((SLOTS + 2,) + BLOCK_SET, jnp.float32),
+    pltpu.VMEM((BLOCKS,) + BLOCK_SET, jnp.float32),
+    pltpu.VMEM((BLOCKS + 1,) + BLOCK_SET, jnp.bfloat16),
+    pltpu.VMEM((BLOCKS + 1,) + BLOCK_SET, jnp.bfloat16),
+    pltpu.VMEM((8, RIM) + BLOCK_SET, jnp.bfloat16),
+    pltpu.VMEM((8, RIM) + BLOCK_SET, jnp.bfloat16),
+    pltpu.VMEM((8, RIM) + BLOCK_SET, jnp.bfloat16),
+    pltpu.VMEM((8, RIM) + BLOCK_SET, jnp.bfloat16),
+    pltpu.VMEM((FULL, 128), jnp.bfloat16),
+    pltpu.VMEM((FULL, 128), jnp.bfloat16),
+    pltpu.SemaphoreType.DMA,
+    pltpu.SemaphoreType.DMA((4, 8)),
+    pltpu.SemaphoreType.DMA((4, 8)),
+]
+
+
+def block_kernel(
+    scale,
+    voxels,
+    first_weight,
+    second_weight,
+    in_slots,
+    out_slots,
+    live_slots,
+    out_grad,
+    result,
+    input_grad,
+    first_grad,
+    second_grad,
+    *scratch,
+):
+    (
+        plan_rows,
+        plan,
+        table_x,
+        table_h,
+        sums,
+        first_sum,
+        first_delta,
+        second_delta,
+        give_h,
+        got_h,
+        give_x,
+        got_x,
+        first_part,
+        second_part,
+        plan_sem,
+        send_sems,
+        recv_sems,
+    ) = scratch[: len(SCRATCH)]
     count = len(Reduce.scratch)
-    both = [
-        Reduce(0, first_part, first_out, scale, *scratch[:count]),
-        Reduce(1, second_part, second_out, scale, *scratch[count:]),
-    ]
-    for step in (
-        "start_core",
-        "start_first",
-        "start_second",
-        "start_owner",
-        "start_result",
-        "start_gather_second",
-        "start_gather_first",
-        "start_gather_core",
-        "finish",
-    ):
-        for one in both:
-            getattr(one, step)()
-
-
-def reduce_all(first_grad, second_grad, scale):
-    def prepared(grad):
-        flat = grad.reshape(ROWS, 128).astype(jnp.bfloat16)
-        return jnp.pad(flat, ((0, FULL - ROWS), (0, 0)))
-
-    shape = jax.ShapeDtypeStruct((FULL, 128), jnp.bfloat16)
-    first, second = pl.pallas_call(
-        functools.partial(reduce_kernel, scale),
-        out_shape=(shape, shape),
-        in_specs=[pl.BlockSpec(memory_space=pltpu.VMEM)] * 2,
-        out_specs=[pl.BlockSpec(memory_space=pltpu.VMEM)] * 2,
-        scratch_shapes=Reduce.scratch * 2,
+    reduces = scratch[len(SCRATCH) :]
+    first = Reduce(0, first_part, first_grad, scale, *reduces[:count])
+    second = Reduce(1, second_part, second_grad, scale, *reduces[count:])
+
+    enter([neighbour(direction) for direction in DIRECTIONS] + group_peers())
+    rim_x = voxels.at[pl.ds(0, RIM)]
+    swap_x = Swap(0, send_sems, recv_sems, [rim_x] * 8, rim_slots(table_x))
+
+    write_plan(in_slots, out_slots, live_slots, plan_rows)
+    copy = pltpu.make_async_copy(plan_rows, plan, plan_sem)
+    copy.start()
+    table_x[:BLOCKS] = voxels[...]
+    zeros = jnp.zeros(BLOCK_SET, jnp.bfloat16)
+    first_delta[BLOCKS] = zeros
+    second_delta[BLOCKS] = zeros
+    sums[0] = jnp.zeros(BLOCK_SET, jnp.float32)
+    for part in (first_part, second_part):
+        part[ROWS:] = jnp.zeros((FULL - ROWS, 128), jnp.bfloat16)
+    copy.wait()
+
+    swap_x.arrive()
+    clear_outside(table_x)
+    convolve(table_x, plan, 0, 2, first_weight, sums, False)
+
+    def hide(block):
+        total = sums[plan[3, block]]
+        first_sum[block] = total
+        table_h[block] = (total * sigmoid(total)).astype(jnp.bfloat16)
+
+    for block in range(RIM):
+        hide(block)
+    rim_h = table_h.at[pl.ds(0, RIM)]
+    swap_h = Swap(1, send_sems, recv_sems, [rim_h] * 8, rim_slots(table_h))
+    pl.loop(RIM, BLOCKS)(hide)
+
+    swap_h.arrive()
+    clear_outside(table_h)
+    convolve(table_h, plan, 0, 2, second_weight, sums, False)
+
+    @pl.loop(0, BLOCKS)
+    def _(block):
+        joined = sums[plan[3, block]] + voxels[block].astype(jnp.float32)
+        result[block] = (joined * sigmoid(joined)).astype(jnp.bfloat16)
+        second_delta[block] = (out_grad[block].astype(jnp.float32) * slope(joined)).astype(
+            jnp.bfloat16
+        )
+
+    def give(buffer):
+        @pl.loop(0, 8)
+        def _(g):
+            for r in range(RIM):
+                buffer[g, r] = sums[plan[5, BLOCKS + RIM * g + r]].astype(jnp.bfloat16)
+
+    def eight(buffer):
+        return [buffer.at[g] for g in range(8)]
+
+    convolve(second_delta, plan, 1, 4, second_weight, sums, True)
+    give(give_h)
+    back_h = Swap(2, send_sems, recv_sems, eight(give_h), eight(got_h))
+
+    def descend(block, total):
+        first_delta[block] = (total * slope(first_sum[block])).astype(jnp.bfloat16)
+
+    @pl.loop(RIM, BLOCKS)
+    def _(block):
+        descend(block, sums[plan[5, block]])
+
+    weight_terms(table_h, second_delta, plan, second_part)
+    second.start_core()
+
+    back_h.arrive()
+    for r in range(RIM):
+        descend(r, routed(sums[plan[5, r]], got_h, r))
+
+    weight_terms(table_x, first_delta, plan, first_part)
+    first.start_core()
+    second.start_first()
+
+    convolve(first_delta, plan, 1, 4, first_weight, sums, True)
+    give(give_x)
+    back_x = Swap(3, send_sems, recv_sems, eight(give_x), eight(got_x))
+    first.start_first()
+    second.start_second()
+
+    def land(block, total):
+        input_grad[block] = (total + second_delta[block].astype(jnp.float32)).astype(jnp.bfloat16)
+
+    @pl.loop(RIM, BLOCKS)
+    def _(block):
+        land(block, sums[plan[5, block]])
+
+    first.start_second()
+    second.start_owner()
+    back_x.arrive()
+    for r in range(RIM):
+        land(r, routed(sums[plan[5, r]], got_x, r))
+
+    first.start_owner()
+    second.start_result()
+    first.start_result()
+    second.start_gather_second()
+    first.start_gather_second()
+    second.start_gather_first()
+    first.start_gather_first()
+    second.start_gather_core()
+    first.start_gather_core()
+    for swap in (swap_x, swap_h, back_h, back_x):
+        swap.finish()
+    second.finish()
+    first.finish()
+
+
+def shards(voxels, first_weight, second_weight, in_slots, out_slots, live_slots, out_grad):
+    tile = (BLOCKS,) + BLOCK_SET
+    scale = 1.0 / math.sqrt(
+        lax.axis_size("gx") * lax.axis_size("gy") * OFFSETS * in_slots.shape[3] * VOXELS
+    )
+    field = jax.ShapeDtypeStruct(tile, jnp.bfloat16)
+    grad = jax.ShapeDtypeStruct((FULL, 128), jnp.bfloat16)
+    result, input_grad, first_grad, second_grad = pl.pallas_call(
+        functools.partial(block_kernel, scale),
+        out_shape=(field, field, grad, grad),
+        in_specs=[pl.BlockSpec(memory_space=pltpu.VMEM)] * 7,
+        out_specs=[pl.BlockSpec(memory_space=pltpu.VMEM)] * 4,
+        scratch_shapes=SCRATCH + Reduce.scratch * 2,
         compiler_params=pltpu.CompilerParams(
-            collective_id=0, has_side_effects=True, vmem_limit_bytes=32 * 1024 * 1024
+            collective_id=0, has_side_effects=True, vmem_limit_bytes=40 * 1024 * 1024
         ),
         cost_estimate=pl.CostEstimate(
-            flops=FULL * 128 * 4, bytes_accessed=8 * FULL * 128, transcendentals=0
+            flops=6 * SLOTS * VOXELS * 128 * 128 * 2,
+            bytes_accessed=4 * FULL * 256,
+            transcendentals=4 * BLOCKS * VOXELS * 128,
         ),
-    )(prepared(first_grad), prepared(second_grad))
-    return first[:ROWS].reshape(27, 128, 128), second[:ROWS].reshape(27, 128, 128)
-
-
-def padded(block, sides, width):
-    for axis, dim in sides:
-        count = lax.axis_size(axis)
-        forward = [(i, i + 1) for i in range(count - 1)]
-        backward = [(target, source) for source, target in forward]
-        low = lax.ppermute(
-            lax.slice_in_dim(block, block.shape[dim] - width, None, axis=dim), axis, forward
-        )
-        high = lax.ppermute(lax.slice_in_dim(block, 0, width, axis=dim), axis, backward)
-        block = jnp.concatenate([low, block, high], axis=dim)
-    return block
-
-
-def smooth_slope(values):
-    sigmoid = jax.nn.sigmoid(values)
-    return sigmoid * (1.0 + values * (1.0 - sigmoid))
-
-
-def share_rim(local):
-    depth = RIM
-    edge = local[:depth][None, None]
-    beside_all = padded(edge, (("gx", 0), ("gy", 1)), 1)
-    beside_all = beside_all.reshape((9, depth) + local.shape[1:])
-    lower = beside_all[:4].reshape((-1,) + local.shape[1:])
-    upper = beside_all[5:].reshape((-1,) + local.shape[1:])
-    return jnp.concatenate([local, lower, upper], axis=0)
-
-
-def return_rim(table_grad, blocks):
-    depth = RIM
-    shape_tail = table_grad.shape[1:]
-    remote = table_grad[blocks:].reshape((8, depth) + shape_tail)
-    middle = jnp.zeros((1, depth) + shape_tail, jnp.float32)
-    layout = jnp.concatenate([remote[:4], middle, remote[4:]], axis=0).reshape(
-        (3, 3, depth) + shape_tail
+    )(
+        voxels.reshape(tile),
+        first_weight,
+        second_weight,
+        in_slots.reshape(in_slots.shape[2:]),
+        out_slots.reshape(in_slots.shape[2:]),
+        live_slots.reshape(in_slots.shape[2:]),
+        out_grad.reshape(tile),
     )
-    along = padded(layout, (("gx", 0),), 1)
-    column = along[0] + along[2] + along[4]
-    across = padded(column, (("gy", 0),), 1)
-    arrived = across[0] + across[2] + across[4]
-    return table_grad[:blocks].at[:depth].add(arrived)
-
-
-def convolve(table, in_rows, out_rows, live_rows, weight, blocks):
-    offsets, slot_count = in_rows.shape
-    voxel_count, width = (table.shape[1], table.shape[2])
-    picked = jnp.take(table, in_rows.reshape(-1), axis=0).reshape(
-        offsets, slot_count * voxel_count, width
-    )
-    product = jnp.einsum("kmc,kcd->kmd", picked, weight, preferred_element_type=jnp.float32)
-    product = product.reshape(offsets * slot_count, voxel_count * width)
-    targets = lax.broadcasted_iota(jnp.int32, (blocks, offsets * slot_count), 0)
-    placing = ((out_rows.reshape(1, -1) == targets) & (live_rows.reshape(1, -1) > 0)).astype(
-        jnp.float32
-    )
-    summed = jnp.dot(
-        placing, product, precision=lax.Precision.HIGHEST, preferred_element_type=jnp.float32
-    )
-    return (summed.reshape(blocks, voxel_count, width), picked)
-
-
-def transpose_conv(delta, picked, in_rows, out_rows, live_rows, weight, table_rows):
-    offsets, slot_count = in_rows.shape
-    voxel_count, width = (delta.shape[1], delta.shape[2])
-    keep = live_rows.reshape(-1, 1, 1).astype(delta.dtype)
-    gathered = (jnp.take(delta, out_rows.reshape(-1), axis=0) * keep).reshape(
-        offsets, slot_count * voxel_count, width
-    )
-    backward = jnp.einsum("kmd,kcd->kmc", gathered, weight, preferred_element_type=jnp.float32)
-    backward = backward.reshape(offsets * slot_count, voxel_count * width)
-    sources = lax.broadcasted_iota(jnp.int32, (table_rows, offsets * slot_count), 0)
-    placing = (in_rows.reshape(1, -1) == sources).astype(jnp.float32)
-    table_grad = jnp.dot(
-        placing, backward, precision=lax.Precision.HIGHEST, preferred_element_type=jnp.float32
-    )
-    weight_grad = jnp.einsum("kmc,kmd->kcd", picked, gathered, preferred_element_type=jnp.float32)
-    return (table_grad.reshape(table_rows, voxel_count, width), weight_grad)
-
-
-def shards(voxels, first_weight, second_weight, in_slots, out_slots, live_slots, out_grad):
-    blocks = voxels.shape[2]
-    shape_tail = voxels.shape[3:]
-    inputs = voxels.reshape((blocks,) + shape_tail)
-    cotangent = out_grad.reshape((blocks,) + shape_tail)
-    in_rows = in_slots.reshape(in_slots.shape[2:])
-    out_rows = out_slots.reshape(out_slots.shape[2:])
-    live_rows = live_slots.reshape(live_slots.shape[2:])
-    table_x = share_rim(inputs)
-    table_rows = table_x.shape[0]
-    first_sum, picked_x = convolve(table_x, in_rows, out_rows, live_rows, first_weight, blocks)
-    hidden = jax.nn.silu(first_sum).astype(jnp.bfloat16)
-    table_h = share_rim(hidden)
-    second_sum, picked_h = convolve(table_h, in_rows, out_rows, live_rows, second_weight, blocks)
-    joined = second_sum + inputs.astype(jnp.float32)
-    result = jax.nn.silu(joined).astype(jnp.bfloat16)
-    second_delta = (cotangent.astype(jnp.float32) * smooth_slope(joined)).astype(jnp.bfloat16)
-    grads_h, second_grad = transpose_conv(
-        second_delta, picked_h, in_rows, out_rows, live_rows, second_weight, table_rows
-    )
-    hidden_grad = return_rim(grads_h, blocks)
-    first_delta = (hidden_grad * smooth_slope(first_sum)).astype(jnp.bfloat16)
-    grads_x, first_grad = transpose_conv(
-        first_delta, picked_x, in_rows, out_rows, live_rows, first_weight, table_rows
-    )
-    input_grad = return_rim(grads_x, blocks) + second_delta.astype(jnp.float32)
-    scale = 1.0 / math.sqrt(
-        lax.axis_size("gx")
-        * lax.axis_size("gy")
-        * in_rows.shape[0]
-        * in_rows.shape[1]
-        * shape_tail[0]
-    )
-    first_grad, second_grad = reduce_all(first_grad, second_grad, scale)
+
+    def unpadded(whole):
+        return whole[:ROWS].reshape(first_weight.shape)
+
     return (
         result.reshape(voxels.shape),
-        input_grad.astype(jnp.bfloat16).reshape(voxels.shape),
-        first_grad,
-        second_grad,
+        input_grad.reshape(voxels.shape),
+        unpadded(first_grad),
+        unpadded(second_grad),
     )
 
 

time: 196 us -> 93.3 us (0.48)
  starting transfers between devices: 45.1 us -> 0 us
  waiting for transfers between devices: 28.1 us -> 0 us
  local copies, waits for them, and re-layouts: 33.6 us -> 9.51 us
  Pallas kernels: 63.8 us -> 82.8 us
  matrix products: 15.6 us -> 0 us
  other arithmetic: 7.02 us -> 0 us
    ppermute x16 -> x0, starting transfers between devices: 45.1 us -> none  [the longest x8 30.1 us: padded(): lax.ppermute(lax.slice_in_dim(block, block.shape[dim] - width, None, axis...]
    ppermute x16 -> x0, waiting for transfers between devices: 28.1 us -> none  [the longest x8 27 us: padded(): lax.ppermute(lax.slice_in_dim(block, 0, width, axis=dim), axis, backward)]
    pallas_call x1, Pallas kernels: 63.8 us -> 82.8 us  [shards(): pl.pallas_call(functools.partial(block_kernel, scale), out_shape=(field,...]
    dot_general x10 -> x0, matrix products: 15.6 us -> none  [the longest x2 4.46 us: transpose_conv(): jnp.dot(placing, backward, precision=lax.Precision.HIGHEST, preferred_ele...]
    reshape x4 -> x3, local copies, waits for them, and re-layouts: 9.67 us -> 0.3 us  [the longest x1 0.1 us: shards(): in_slots.reshape(in_slots.shape[2:])]
    unnamed x59 -> x16, local copies, waits for them, and re-layouts: 12.2 us -> 7.28 us
    gather x4 -> x0, local copies, waits for them, and re-layouts: 4.62 us -> none  [the longest x2 3.18 us: transpose_conv(): jnp.take(delta, out_rows.reshape(-1), axis=0) * keep]
    slice x16 -> x2, local copies, waits for them, and re-layouts: 5.09 us -> 1.94 us  [unpadded(): return whole[:ROWS].reshape(first_weight.shape)]
  transfers between devices with their start and end apart: 16 -> 0, of which waited for: 8 -> 0; matrix products, arithmetic and copies ran while one was open for 6% -> 0% of each run, Pallas kernels for 33% -> 0%
where the time goes in v2:
time: 93.3 us; the launch traced here: 93 us
  Pallas kernels  82.8 us (89%)
  local copies, waits for them, and re-layouts  9.51 us (10%)
    pallas_call x1, Pallas kernels, shards(): pl.pallas_call(functools.partial(block_kernel, scale), out_shape=(field,...  82.8 us
    unnamed x16, local copies, waits for them, and re-layouts  7.28 us
    slice x2, local copies, waits for them, and re-layouts, unpadded(): return whole[:ROWS].reshape(first_weight.shape)  1.94 us

profile of v2, /device:TPU:1, one launch (start us, length us, event | category | flops | bytes accessed | tf_op | source)
XLA Modules:
  0.0 93.0 jit_solution(15497328192051559499)
XLA Ops:
  0.6 0.0 copy-start.4
  0.6 0.7 copy-done.4
  1.3 0.0 copy-start.5
  1.3 0.1 copy.11.in_slots
  1.4 0.6 copy-done.5
  2.0 0.0 copy-start.6
  2.0 0.1 copy.12.out_slots
  2.1 0.6 copy-done.6
  2.7 0.1 copy.13.live_slots
  2.8 0.0 copy-start
  2.8 1.2 %copy-done = bf16[27,128,128]{2,1,0:T(8,128)(2,1)S(1)} copy-done((bf16[27,128,128]{2,1,0:T(8,128)(2,1)S(1)}, bf16[27,128,128]{2,1,0:T(8,128)(2,1)}, u32[]{:S(2)}) %copy-start) | copy-done | bytes 884760
  3.9 0.0 copy-start.1
  3.9 1.2 %copy-done.1 = bf16[27,128,128]{2,1,0:T(8,128)(2,1)S(1)} copy-done((bf16[27,128,128]{2,1,0:T(8,128)(2,1)S(1)}, bf16[27,128,128]{2,1,0:T(8,128)(2,1)}, u32[]{:S(2)}) %copy-start.1) | copy-done | bytes 884760
  5.1 0.0 copy-start.2
  5.1 0.9 copy-done.2
  6.0 0.0 copy-start.3
  6.0 0.9 copy-done.3
  6.9 82.8 %shard_map.102 = (bf16[8,64,128]{2,1,0:T(8,128)(2,1)S(1)}, bf16[8,64,128]{2,1,0:T(8,128)(2,1)S(1)}, bf16[3584,128]{1,0:T(8,128)(2,1)S(1)}, bf16[3584,128]{1,0:T(8,128)(2,1)S(1)}) custom-call(bf16[8,64,128]{2,1,0:T(8,128)(2,1)S(1)} %bitcast.11, bf16[27,128,128]{2,1,0:T(8,128)(2,1)S(1)} %copy-done, bf16[27,128,128]{2,1,0:T(8,128)(2,1)S(1)} %copy-done.1, ...), custom_call_target="tpu_custom_call" | custom-call | flops 679477248 | bytes 3670016 | tf_op jit(solution)/shard_map/pallas_call | solution.py:606
  89.7 1.0 %slice.6 = bf16[3456,128]{1,0:T(8,128)(2,1)} slice(bf16[3584,128]{1,0:T(8,128)(2,1)S(1)} %get-tuple-element.10), slice={[0:3456], [0:128]} | slice | bytes 1769472 | tf_op jit(solution)/shard_map/slice | solution.py:631
  90.7 1.0 %slice.7 = bf16[3456,128]{1,0:T(8,128)(2,1)} slice(bf16[3584,128]{1,0:T(8,128)(2,1)S(1)} %get-tuple-element.11), slice={[0:3456], [0:128]} | slice | bytes 1769472 | tf_op jit(solution)/shard_map/slice | solution.py:631
  91.7 0.7 copy.16
  92.3 0.7 copy.17
Async XLA Ops:
  0.6 0.7 copy-start.4
  1.3 0.7 copy-start.5
  2.0 0.7 copy-start.6
  2.8 1.2 %copy-start = (bf16[27,128,128]{2,1,0:T(8,128)(2,1)S(1)}, bf16[27,128,128]{2,1,0:T(8,128)(2,1)}, u32[]{:S(2)}) copy-start(bf16[27,128,128]{2,1,0:T(8,128)(2,1)} %first_weight.1) | copy-start | bytes 2654212
  3.9 1.2 %copy-start.1 = (bf16[27,128,128]{2,1,0:T(8,128)(2,1)S(1)}, bf16[27,128,128]{2,1,0:T(8,128)(2,1)}, u32[]{:S(2)}) copy-start(bf16[27,128,128]{2,1,0:T(8,128)(2,1)} %second_weight.1) | copy-start | bytes 2654212
  5.1 0.9 copy-start.2
  6.0 0.9 copy-start.3

commit v3 on v2

v3 whole, which is shorter than its diff:
```python
import functools
import math

import jax
import jax.numpy as jnp
from jax import lax
from jax.experimental import pallas as pl
from jax.experimental.pallas import tpu as pltpu
from jax.sharding import PartitionSpec as P

RIM = 2
MESH = pl.DeviceIdType.MESH

ROWS = 27 * 128
HALF = 1792
FULL = 2 * HALF
HALF_OFFSETS = HALF // 128
PIECE = HALF // 16
QUARTER = 32


def rows(start, size):
    return pl.ds(pl.multiple_of(start, 16), size)


def place():
    gx, gy = lax.axis_index("gx"), lax.axis_index("gy")
    core = lax.rem(gx, 2)
    x = lax.rem(gx // 2, 2) * 2 + gy // 4
    return gx // 4, x, lax.rem(gy, 4), core


def device(z, x, y, core):
    return ((z * 2 + x // 2) * 2 + core, lax.rem(x, 2) * 4 + y)


def partner():
    z, x, y, core = place()
    return device(z, x, y, 1 - core)


def hops(d):
    return min(d // 4, 4 - d // 4) + min(d % 4, 4 - d % 4)


PLANE = sorted(range(1, 16), key=lambda d: -hops(d))


def in_plane(d):
    z, x, y, core = place()
    return device(z, lax.rem(x + d // 4, 4), lax.rem(y + d % 4, 4), core)


def plane_index(d):
    _, x, y, _ = place()
    return lax.rem(x + d // 4, 4) * 4 + lax.rem(y + d % 4, 4)


def opposite(d):
    return (4 - d // 4) % 4 * 4 + (4 - d % 4) % 4


def near(d):
    z, x, y, core = place()
    index = lax.rem(z + d, 4)
    return index, device(z // 4 * 4 + index, x, y, core)


def far(d):
    z, x, y, core = place()
    return device(lax.rem(z + 4 * d, 16), x, y, core)


class Reduce:
    scratch = [
        pltpu.VMEM((HALF, 128), jnp.bfloat16),
        pltpu.VMEM((15, PIECE, 128), jnp.bfloat16),
        pltpu.VMEM((4 * QUARTER, 128), jnp.bfloat16),
        pltpu.VMEM((3, QUARTER, 128), jnp.bfloat16),
        pltpu.VMEM((4, QUARTER, 128), jnp.bfloat16),
        pltpu.VMEM((4 * QUARTER, 128), jnp.bfloat16),
        pltpu.SemaphoreType.DMA((2, 16)),
        pltpu.SemaphoreType.DMA((2, 4)),
        pltpu.SemaphoreType.DMA((2, 4)),
        pltpu.SemaphoreType.DMA((2, 4)),
        pltpu.SemaphoreType.DMA((2, 16)),
        pltpu.SemaphoreType.DMA((2, 16)),
    ]

    def __init__(self, out, scale, *scratch):
        self.out, self.scale = out, scale
        (
            self.part,
            self.got_plane,
            self.plane_sum,
            self.got_near,
            self.fars,
            self.whole,
            self.plane_sems,
            self.near_sems,
            self.far_sems,
            self.back_sems,
            self.gather_sems,
            self.core_sems,
        ) = scratch
        self.sent = []

    def clear(self):
        self.plane_sum[PIECE:] = jnp.zeros((4 * QUARTER - PIECE, 128), jnp.bfloat16)

    def send(self, src, dst, sems, index, device_id):
        copy = pltpu.make_async_remote_copy(
            src_ref=src,
            dst_ref=dst,
            send_sem=sems.at[0, index],
            recv_sem=sems.at[1, index],
            device_id=device_id,
            device_id_type=MESH,
        )
        copy.start()
        self.sent.append(copy)

    def arrive(self, dst, sems, index):
        pltpu.make_async_copy(dst, dst, sems.at[1, index]).wait()

    def start_plane(self):
        for d in PLANE:
            self.send(
                self.part.at[rows(plane_index(d) * PIECE, PIECE)],
                self.got_plane.at[d - 1],
                self.plane_sems,
                d,
                in_plane(d),
            )

    def start_near(self):
        total = self.part[rows(plane_index(0) * PIECE, PIECE)].astype(jnp.float32)
        for d in reversed(PLANE):
            self.arrive(self.got_plane.at[d - 1], self.plane_sems, d)
            total = total + self.got_plane[d - 1].astype(jnp.float32)
        self.plane_sum[:PIECE] = total.astype(jnp.bfloat16)
        for d in (2, 1, 3):
            index, target = near(d)
            self.send(
                self.plane_sum.at[rows(index * QUARTER, QUARTER)],
                self.got_near.at[d - 1],
                self.near_sems,
                d,
                target,
            )

    def start_far(self):
        index, _ = near(0)
        total = self.plane_sum[rows(index * QUARTER, QUARTER)].astype(jnp.float32)
        for d in (1, 2, 3):
            self.arrive(self.got_near.at[d - 1], self.near_sems, d)
            total = total + self.got_near[d - 1].astype(jnp.float32)
        group = place()[0] // 4
        self.fars[group] = total.astype(jnp.bfloat16)
        for d in (2, 1, 3):
            self.send(self.fars.at[group], self.fars.at[group], self.far_sems, d, far(d))

    def start_back(self):
        group = place()[0] // 4
        for d in (1, 3, 2):
            self.arrive(self.fars.at[lax.rem(group + 4 - d, 4)], self.far_sems, d)
        total = self.fars[0].astype(jnp.float32)
        for other in (1, 2, 3):
            total = total + self.fars[other].astype(jnp.float32)
        index, _ = near(0)
        piece = rows(index * QUARTER, QUARTER)
        self.whole[piece] = (total * self.scale).astype(jnp.bfloat16)
        for d in (2, 1, 3):
            self.send(self.whole.at[piece], self.whole.at[piece], self.back_sems, d, near(d)[1])

    def spot(self, d, core):
        return self.out.at[rows(core * HALF + plane_index(d) * PIECE, PIECE)]

    def start_gather(self):
        for d in (1, 3, 2):
            piece = self.whole.at[rows(near(4 - d)[0] * QUARTER, QUARTER)]
            self.arrive(piece, self.back_sems, d)
        core = place()[3]
        own = self.spot(0, core)
        own[...] = self.whole[:PIECE]
        for d in PLANE:
            self.send(own, own, self.gather_sems, d, in_plane(d))
        self.send(own, own, self.core_sems, 0, partner())

    def start_core(self):
        core = place()[3]
        for d in reversed(PLANE):
            piece = self.spot(opposite(d), core)
            self.arrive(piece, self.gather_sems, d)
            self.send(piece, piece, self.core_sems, d, partner())

    def finish(self):
        core = place()[3]
        for d in range(16):
            self.arrive(self.spot(opposite(d), 1 - core), self.core_sems, d)
        for copy in self.sent:
            copy.wait_send()


def enter(peers):
    barrier = pltpu.get_barrier_semaphore()
    for peer in peers:
        pl.semaphore_signal(barrier, inc=1, device_id=peer, device_id_type=MESH)
    pl.semaphore_wait(barrier, len(peers))


BLOCKS, VOXELS, OFFSETS, SLOTS, TABLE = 8, 64, 27, 54, 24
DIRECTIONS = [(a, b) for a in (-1, 0, 1) for b in (-1, 0, 1) if (a, b) != (0, 0)]


def neighbour(direction):
    a, b = direction
    gx, gy = lax.axis_index("gx"), lax.axis_index("gy")
    return lax.rem(gx + a + 64, 64), lax.rem(gy + b + 8, 8)


def present(direction):
    a, b = direction
    gx, gy = lax.axis_index("gx") + a, lax.axis_index("gy") + b
    return (gx >= 0) & (gx < 64) & (gy >= 0) & (gy < 8)


def sigmoid(values):
    return 1.0 / (1.0 + jnp.exp(-values))


def slope(values):
    s = sigmoid(values)
    return s * (1.0 + values * (1.0 - s))


IN, DELTA, OUT_CHAIN, OUT_LAST, IN_CHAIN, IN_LAST = 0, 2, 4, 6, 8, 10


def write_plan(in_ref, out_ref, live_ref, plan):
    shape = (OFFSETS, OFFSETS)
    lane = lax.broadcasted_iota(jnp.int32, shape, 1)
    offset = lax.broadcasted_iota(jnp.int32, shape, 0)

    def across(values, s):
        return jnp.broadcast_to(values[s : s + 1], shape)

    def down(values, s):
        picked = jnp.where(lane == offset, across(values, s), -1)
        return jnp.broadcast_to(jnp.max(picked, axis=1, keepdims=True), shape)

    def chain(values, row, last_row):
        columns = [down(values, s) for s in (0, 1)]
        last = jnp.zeros(shape, jnp.int32)
        for s in (0, 1):
            target = across(values, s)
            found = jnp.zeros(shape, jnp.int32)
            for t in (0, 1):
                earlier = 2 * offset + t < 2 * lane + s
                same = (columns[t] == target) & earlier & (target >= 0)
                found = jnp.maximum(found, jnp.where(same, 2 * offset + t + 1, 0))
            last = jnp.maximum(last, jnp.where(columns[s] == lane, 2 * offset + s + 1, 0))
            plan[row + s : row + s + 1, :OFFSETS] = jnp.max(found, axis=0, keepdims=True)
        plan[last_row : last_row + 1, :OFFSETS] = jnp.max(last, axis=0, keepdims=True)

    plan[...] = jnp.zeros_like(plan)
    source, target, live = in_ref[...], out_ref[...], live_ref[...]
    plan[IN : IN + 2, :OFFSETS] = source
    plan[DELTA : DELTA + 2, :OFFSETS] = jnp.where(live > 0, target, BLOCKS)
    chain(jnp.where(live > 0, target, -1), OUT_CHAIN, OUT_LAST)
    chain(jnp.where(live > 0, source, -1), IN_CHAIN, IN_LAST)


UNROLL = 9


def step_loop(count, body, unroll=None):
    unroll = unroll or UNROLL
    unroll = max(u for u in range(1, unroll + 1) if count % u == 0)

    @pl.loop(0, count // unroll)
    def _(step):
        for u in range(unroll):
            body(step * unroll + u)


def pair_of(table, plan, row, k):
    return [table[plan[row, k]], table[plan[row + 1, k]]]


def convolve(table, plan, row, chain, weight, sums, flipped):
    def body(k):
        product = lax.dot_general(
            jnp.concatenate(pair_of(table, plan, row, k), axis=0),
            weight[k],
            (((1,), (1 if flipped else 0,)), ((), ())),
            preferred_element_type=jnp.float32,
        )
        sums[2 * k + 1] = sums[plan[chain, k]] + product[:VOXELS]
        sums[2 * k + 2] = sums[plan[chain + 1, k]] + product[VOXELS:]

    step_loop(OFFSETS, body)


def weight_terms(tables, deltas, plans, part):
    core = place()[3]

    def body(j):
        k = jnp.minimum(core * HALF_OFFSETS + j, OFFSETS - 1)
        left, right = [], []
        for table, delta, plan in zip(tables, deltas, plans):
            left += pair_of(table, plan, IN, k)
            right += pair_of(delta, plan, DELTA, k)
        product = lax.dot_general(
            jnp.concatenate(left, axis=0),
            jnp.concatenate(right, axis=0),
            (((0,), (0,)), ((), ())),
            preferred_element_type=jnp.float32,
        )
        part[rows(j * 128, 128)] = product.astype(jnp.bfloat16)

    step_loop(HALF_OFFSETS, body, 7)


class Swap:
    def __init__(self, index, send_sems, recv_sems, sources, targets):
        self.copies = []
        for g, direction in enumerate(DIRECTIONS):
            copy = pltpu.make_async_remote_copy(
                src_ref=sources[g],
                dst_ref=targets[7 - g],
                send_sem=send_sems.at[index, g],
                recv_sem=recv_sems.at[index, 7 - g],
                device_id=neighbour(direction),
                device_id_type=MESH,
            )
            copy.start()
            self.copies.append(copy)

    def arrive(self):
        for copy in self.copies:
            copy.wait_recv()

    def finish(self):
        for copy in self.copies:
            copy.wait_send()


def rim_slots(table):
    return [table.at[pl.ds(BLOCKS + RIM * g, RIM)] for g in range(8)]


def clear_outside(table):
    for g, direction in enumerate(DIRECTIONS):

        @pl.when(jnp.logical_not(present(direction)))
        def _():
            table[BLOCKS + RIM * g : BLOCKS + RIM * (g + 1)] = jnp.zeros(
                (RIM, VOXELS, 128), jnp.bfloat16
            )


def routed(own, arrived, r):
    total = own
    for g, direction in enumerate(DIRECTIONS):
        total = total + jnp.where(present(direction), arrived[g, r].astype(jnp.float32), 0.0)
    return total


BLOCK_SET = (VOXELS, 128)
SCRATCH = [
    pltpu.VMEM((2, OFFSETS), jnp.int32),
    pltpu.VMEM((2, OFFSETS), jnp.int32),
    pltpu.VMEM((2, OFFSETS), jnp.int32),
    pltpu.VMEM((OFFSETS, 128, 128), jnp.bfloat16),
    pltpu.VMEM((OFFSETS, 128, 128), jnp.bfloat16),
    pltpu.VMEM((BLOCKS,) + BLOCK_SET, jnp.bfloat16),
    pltpu.VMEM((16, 128), jnp.int32),
    pltpu.VMEM((16, 128), jnp.int32),
    pltpu.SMEM((16, 128), jnp.int32),
    pltpu.SMEM((16, 128), jnp.int32),
    pltpu.VMEM((TABLE,) + BLOCK_SET, jnp.bfloat16),
    pltpu.VMEM((TABLE,) + BLOCK_SET, jnp.bfloat16),
    pltpu.VMEM((TABLE,) + BLOCK_SET, jnp.bfloat16),
    pltpu.VMEM((TABLE,) + BLOCK_SET, jnp.bfloat16),
    pltpu.VMEM((2 * OFFSETS + 2,) + BLOCK_SET, jnp.float32),
    pltpu.VMEM((BLOCKS,) + BLOCK_SET, jnp.float32),
    pltpu.VMEM((BLOCKS + 1,) + BLOCK_SET, jnp.bfloat16),
    pltpu.VMEM((BLOCKS + 1,) + BLOCK_SET, jnp.bfloat16),
    pltpu.VMEM((BLOCKS + 1,) + BLOCK_SET, jnp.bfloat16),
    pltpu.VMEM((BLOCKS + 1,) + BLOCK_SET, jnp.bfloat16),
    pltpu.VMEM((8, RIM) + BLOCK_SET, jnp.bfloat16),
    pltpu.VMEM((8, RIM) + BLOCK_SET, jnp.bfloat16),
    pltpu.VMEM((8, RIM) + BLOCK_SET, jnp.bfloat16),
    pltpu.VMEM((8, RIM) + BLOCK_SET, jnp.bfloat16),
    pltpu.SemaphoreType.DMA((9,)),
    pltpu.SemaphoreType.DMA((2, 8)),
    pltpu.SemaphoreType.DMA((4, 8)),
    pltpu.SemaphoreType.DMA((4, 8)),
]


def block_kernel(
    scale,
    voxels_in,
    first_weight_in,
    second_weight_in,
    in_slots,
    out_slots,
    live_slots,
    out_grad_in,
    result,
    input_grad,
    first_grad,
    second_grad,
    *scratch,
):
    (
        in_rows,
        out_rows,
        live_rows,
        first_weight,
        second_weight,
        out_grad,
        plan_rows,
        other_rows,
        plan,
        other_plan,
        table_x,
        table_h,
        other_x,
        other_h,
        sums,
        first_sum,
        first_delta,
        second_delta,
        other_first,
        other_second,
        give_h,
        got_h,
        give_x,
        got_x,
        load_sems,
        core_sems,
        send_sems,
        recv_sems,
    ) = scratch[: len(SCRATCH)]
    count = len(Reduce.scratch)
    reduces = scratch[len(SCRATCH) :]
    first = Reduce(first_grad, scale, *reduces[:count])
    second = Reduce(second_grad, scale, *reduces[count:])
    to_core = []

    def load(index, src, dst):
        copy = pltpu.make_async_copy(src, dst, load_sems.at[index])
        copy.start()
        return copy

    def share(index, src, dst):
        copy = pltpu.make_async_remote_copy(
            src_ref=src,
            dst_ref=dst,
            send_sem=core_sems.at[0, index],
            recv_sem=core_sems.at[1, index],
            device_id=partner(),
            device_id_type=MESH,
        )
        copy.start()
        to_core.append(copy)
        return copy

    own = table_x.at[pl.ds(0, BLOCKS)]
    load_x = load(0, voxels_in, own)
    load_slots = [
        load(1, in_slots, in_rows),
        load(2, out_slots, out_rows),
        load(3, live_slots, live_rows),
    ]
    load_first = load(4, first_weight_in, first_weight)
    load_second = load(5, second_weight_in, second_weight)
    load_grad = load(6, out_grad_in, out_grad)

    others = [far(d) for d in (2, 1, 3)] + [near(d)[1] for d in (1, 2, 3)]
    others += [neighbour(direction) for direction in DIRECTIONS]
    others += [in_plane(d) for d in PLANE] + [partner()]
    enter(others)
    load_x.wait()
    rim_x = table_x.at[pl.ds(0, RIM)]
    swap_x = Swap(0, send_sems, recv_sems, [rim_x] * 8, rim_slots(table_x))

    for copy in load_slots:
        copy.wait()
    write_plan(in_rows, out_rows, live_rows, plan_rows)
    load_plan = load(7, plan_rows, plan)
    share_plan = share(0, plan_rows, other_rows)
    zeros = jnp.zeros(BLOCK_SET, jnp.bfloat16)
    for delta in (first_delta, second_delta, other_first, other_second):
        delta[BLOCKS] = zeros
    sums[0] = jnp.zeros(BLOCK_SET, jnp.float32)
    first.clear()
    second.clear()
    load_plan.wait()
    share_plan.wait_recv()
    load_other = load(8, other_rows, other_plan)
    load_first.wait()

    swap_x.arrive()
    clear_outside(table_x)
    share_x = share(1, table_x, other_x)
    convolve(table_x, plan, IN, OUT_CHAIN, first_weight, sums, False)

    def hide(block):
        total = sums[plan[OUT_LAST, block]]
        first_sum[block] = total
        table_h[block] = (total * sigmoid(total)).astype(jnp.bfloat16)

    for block in range(RIM):
        hide(block)
    rim_h = table_h.at[pl.ds(0, RIM)]
    swap_h = Swap(1, send_sems, recv_sems, [rim_h] * 8, rim_slots(table_h))
    pl.loop(RIM, BLOCKS)(hide)

    load_other.wait()
    load_second.wait()
    load_grad.wait()
    swap_h.arrive()
    clear_outside(table_h)
    share_h = share(2, table_h, other_h)
    convolve(table_h, plan, IN, OUT_CHAIN, second_weight, sums, False)

    @pl.loop(0, BLOCKS)
    def _(block):
        joined = sums[plan[OUT_LAST, block]] + table_x[block].astype(jnp.float32)
        gate = sigmoid(joined)
        result[block] = (joined * gate).astype(jnp.bfloat16)
        second_delta[block] = (
            out_grad[block].astype(jnp.float32) * (gate * (1.0 + joined * (1.0 - gate)))
        ).astype(jnp.bfloat16)

    def all_of(delta, first_block, last_block):
        return delta.at[pl.ds(first_block, last_block - first_block)]

    share_second = share(
        3, all_of(second_delta, 0, BLOCKS), all_of(other_second, 0, BLOCKS)
    )

    def give(buffer):
        @pl.loop(0, 8)
        def _(g):
            for r in range(RIM):
                buffer[g, r] = sums[plan[IN_LAST, BLOCKS + RIM * g + r]].astype(jnp.bfloat16)

    def eight(buffer):
        return [buffer.at[g] for g in range(8)]

    convolve(second_delta, plan, DELTA, IN_CHAIN, second_weight, sums, True)
    give(give_h)
    back_h = Swap(2, send_sems, recv_sems, eight(give_h), eight(got_h))

    def descend(block, total):
        first_delta[block] = (total * slope(first_sum[block])).astype(jnp.bfloat16)

    @pl.loop(RIM, BLOCKS)
    def _(block):
        descend(block, sums[plan[IN_LAST, block]])

    share_inner = share(
        4, all_of(first_delta, RIM, BLOCKS), all_of(other_first, RIM, BLOCKS)
    )
    share_h.wait_recv()
    share_second.wait_recv()
    weight_terms(
        (table_h, other_h), (second_delta, other_second), (plan, other_plan), second.part
    )
    second.start_plane()

    back_h.arrive()
    for r in range(RIM):
        descend(r, routed(sums[plan[IN_LAST, r]], got_h, r))
    share_rim = share(5, all_of(first_delta, 0, RIM), all_of(other_first, 0, RIM))
    share_x.wait_recv()
    share_inner.wait_recv()
    share_rim.wait_recv()
    weight_terms((table_x, other_x), (first_delta, other_first), (plan, other_plan), first.part)
    first.start_plane()

    convolve(first_delta, plan, DELTA, IN_CHAIN, first_weight, sums, True)
    give(give_x)
    back_x = Swap(3, send_sems, recv_sems, eight(give_x), eight(got_x))
    second.start_near()

    def land(block, total):
        input_grad[block] = (total + second_delta[block].astype(jnp.float32)).astype(jnp.bfloat16)

    @pl.loop(RIM, BLOCKS)
    def _(block):
        land(block, sums[plan[IN_LAST, block]])

    second.start_far()
    first.start_near()
    back_x.arrive()
    for r in range(RIM):
        land(r, routed(sums[plan[IN_LAST, r]], got_x, r))
    first.start_far()
    second.start_back()
    first.start_back()
    second.start_gather()
    first.start_gather()
    second.start_core()
    first.start_core()
    for copy in to_core:
        copy.wait_send()
    for swap in (swap_x, swap_h, back_h, back_x):
        swap.finish()
    second.finish()
    first.finish()


def place_kernel(*refs):
    sems = refs[-1]
    copies = []
    for index in range(4):
        copy = pltpu.make_async_copy(refs[index], refs[4 + index], sems.at[index])
        copy.start()
        copies.append(copy)
    for copy in copies:
        copy.wait()


def shards(voxels, first_weight, second_weight, in_slots, out_slots, live_slots, out_grad):
    tile = (BLOCKS,) + BLOCK_SET
    scale = 1.0 / math.sqrt(
        lax.axis_size("gx") * lax.axis_size("gy") * OFFSETS * in_slots.shape[3] * VOXELS
    )
    field = jax.ShapeDtypeStruct(tile, jnp.bfloat16)
    grad = jax.ShapeDtypeStruct((FULL, 128), jnp.bfloat16)
    vmem, hbm = (pl.BlockSpec(memory_space=space) for space in (pltpu.VMEM, pltpu.HBM))

    def slots(values):
        return values.reshape(values.shape[2:]).T

    def in_hbm(*values):
        return [pltpu.with_memory_space_constraint(value, pltpu.HBM) for value in values]

    outputs = pl.pallas_call(
        functools.partial(block_kernel, scale),
        out_shape=(field, field, grad, grad),
        in_specs=[hbm] * 7,
        out_specs=[vmem] * 4,
        scratch_shapes=SCRATCH + Reduce.scratch * 2,
        compiler_params=pltpu.CompilerParams(
            collective_id=0, has_side_effects=True, vmem_limit_bytes=48 * 1024 * 1024
        ),
        cost_estimate=pl.CostEstimate(
            flops=6 * 54 * VOXELS * 128 * 128 * 2,
            bytes_accessed=4 * FULL * 256,
            transcendentals=4 * BLOCKS * VOXELS * 128,
        ),
        name="block",
    )(
        *in_hbm(
            voxels.reshape(tile),
            first_weight,
            second_weight,
            slots(in_slots),
            slots(out_slots),
            slots(live_slots),
            out_grad.reshape(tile),
        )
    )
    whole = jax.ShapeDtypeStruct((ROWS, 128), jnp.bfloat16)
    result, input_grad, first_grad, second_grad = pl.pallas_call(
        lambda *refs: place_kernel(
            refs[0], refs[1], refs[2].at[pl.ds(0, ROWS)], refs[3].at[pl.ds(0, ROWS)], *refs[4:]
        ),
        out_shape=(field, field, whole, whole),
        in_specs=[vmem] * 4,
        out_specs=[hbm] * 4,
        scratch_shapes=[pltpu.SemaphoreType.DMA((4,))],
        compiler_params=pltpu.CompilerParams(vmem_limit_bytes=1024 * 1024),
        name="place",
    )(*outputs)
    return (
        result.reshape(voxels.shape),
        input_grad.reshape(voxels.shape),
        first_grad.reshape(first_weight.shape),
        second_grad.reshape(first_weight.shape),
    )


def solution(mesh):
    return jax.shard_map(
        shards,
        mesh=mesh,
        in_specs=(
            P("gx", "gy", None, None, None),
            P(),
            P(),
            P("gx", "gy", None, None),
            P("gx", "gy", None, None),
            P("gx", "gy", None, None),
            P("gx", "gy", None, None, None),
        ),
        out_specs=(P("gx", "gy", None, None, None), P("gx", "gy", None, None, None), P(), P()),
        check_vma=False,
    )
```

time: 93.3 us -> 76 us (0.81)
  local copies, waits for them, and re-layouts: 9.51 us -> 0 us
  Pallas kernels: 82.8 us -> 75.2 us
    pallas_call x1, Pallas kernels: 82.8 us -> 73.9 us  [shards(): pl.pallas_call(functools.partial(block_kernel, scale), out_shape=(field,...]
    unnamed x16 -> x0, local copies, waits for them, and re-layouts: 7.28 us -> none
    slice x2 -> x0, local copies, waits for them, and re-layouts: 1.94 us -> none  [unpadded(): return whole[:ROWS].reshape(first_weight.shape)]
    pallas_call x0 -> x1, Pallas kernels: none -> 1.33 us  [shards(): pl.pallas_call(lambda *refs: place_kernel(refs[0], refs[1], refs[2].at[pl...]
where the time goes in v3:
time: 76 us; the launch traced here: 75.9 us
  Pallas kernels  75.2 us (99%)
    pallas_call x1, Pallas kernels, shards(): pl.pallas_call(functools.partial(block_kernel, scale), out_shape=(field,...  73.9 us

profile of v3, /device:TPU:1, one launch (start us, length us, event | category | flops | bytes accessed | tf_op | source)
XLA Modules:
  0.0 75.9 jit_solution(5855437207487905372)
XLA Ops:
  0.6 73.9 %block.1 = (bf16[8,64,128]{2,1,0:T(8,128)(2,1)S(1)}, bf16[8,64,128]{2,1,0:T(8,128)(2,1)S(1)}, bf16[3584,128]{1,0:T(8,128)(2,1)S(1)}, bf16[3584,128]{1,0:T(8,128)(2,1)S(1)}) custom-call(bf16[8,64,128]{2,1,0:T(8,128)(2,1)} %bitcast.17, bf16[27,128,128]{2,1,0:T(8,128)(2,1)} %first_weight_in.1, bf16[27,128,128]{2,1,0:T(8,128)(2,1)} %second_weight_in.1, ...), custom_call_target="tpu_custom_call" | custom-call | flops 679477248 | bytes 3670016 | tf_op jit(solution)/shard_map/block/pallas_call | solution.py:645
  74.5 1.3 %place.1 = (bf16[8,64,128]{2,1,0:T(8,128)(2,1)}, bf16[8,64,128]{2,1,0:T(8,128)(2,1)}, bf16[3456,128]{1,0:T(8,128)(2,1)}, bf16[3456,128]{1,0:T(8,128)(2,1)}) custom-call(bf16[8,64,128]{2,1,0:T(8,128)(2,1)S(1)} %get-tuple-element.12.refs_0_, bf16[8,64,128]{2,1,0:T(8,128)(2,1)S(1)} %get-tuple-element.13.refs_1_, ...), custom_call_target="tpu_custom_call" | custom-call | tf_op jit(solution)/shard_map/place/pallas_call | solution.py:672

commit v4 on v3

--- a/solution.py
+++ b/solution.py
@@ -64,6 +64,11 @@
     z, x, y, core = place()
     index = lax.rem(z + d, 4)
     return index, device(z // 4 * 4 + index, x, y, core)
+
+
+def ring(d):
+    z, x, y, core = place()
+    return device(lax.rem(z + d + 16, 16), x, y, core)
 
 
 def far(d):
@@ -120,6 +125,11 @@
         copy.start()
         self.sent.append(copy)
 
+    def drain(self):
+        for copy in self.sent:
+            copy.wait_send()
+        self.sent = []
+
     def arrive(self, dst, sems, index):
         pltpu.make_async_copy(dst, dst, sems.at[1, index]).wait()
 
@@ -139,6 +149,7 @@
             self.arrive(self.got_plane.at[d - 1], self.plane_sems, d)
             total = total + self.got_plane[d - 1].astype(jnp.float32)
         self.plane_sum[:PIECE] = total.astype(jnp.bfloat16)
+        before, self.sent = self.sent, []
         for d in (2, 1, 3):
             index, target = near(d)
             self.send(
@@ -148,6 +159,8 @@
                 d,
                 target,
             )
+        for copy in before:
+            copy.wait_send()
 
     def start_far(self):
         index, _ = near(0)
@@ -183,9 +196,12 @@
         core = place()[3]
         own = self.spot(0, core)
         own[...] = self.whole[:PIECE]
+        before, self.sent = self.sent, []
         for d in PLANE:
             self.send(own, own, self.gather_sems, d, in_plane(d))
         self.send(own, own, self.core_sems, 0, partner())
+        for copy in before:
+            copy.wait_send()
 
     def start_core(self):
         core = place()[3]
@@ -198,8 +214,7 @@
         core = place()[3]
         for d in range(16):
             self.arrive(self.spot(opposite(d), 1 - core), self.core_sems, d)
-        for copy in self.sent:
-            copy.wait_send()
+        self.drain()
 
 
 def enter(peers):
@@ -397,6 +412,7 @@
     pltpu.SemaphoreType.DMA((2, 8)),
     pltpu.SemaphoreType.DMA((4, 8)),
     pltpu.SemaphoreType.DMA((4, 8)),
+    pltpu.SemaphoreType.REGULAR((3,)),
 ]
 
 
@@ -444,6 +460,7 @@
         core_sems,
         send_sems,
         recv_sems,
+        reach,
     ) = scratch[: len(SCRATCH)]
     count = len(Reduce.scratch)
     reduces = scratch[len(SCRATCH) :]
@@ -480,13 +497,19 @@
     load_second = load(5, second_weight_in, second_weight)
     load_grad = load(6, out_grad_in, out_grad)
 
-    others = [far(d) for d in (2, 1, 3)] + [near(d)[1] for d in (1, 2, 3)]
-    others += [neighbour(direction) for direction in DIRECTIONS]
-    others += [in_plane(d) for d in PLANE] + [partner()]
-    enter(others)
+    def signal_reach(step):
+        for d in (1 << step, -(1 << step)):
+            pl.semaphore_signal(reach.at[step], inc=1, device_id=ring(d), device_id_type=MESH)
+
+    enter(
+        [neighbour(direction) for direction in DIRECTIONS]
+        + [in_plane(d) for d in PLANE]
+        + [ring(1), ring(-1), partner()]
+    )
     load_x.wait()
     rim_x = table_x.at[pl.ds(0, RIM)]
     swap_x = Swap(0, send_sems, recv_sems, [rim_x] * 8, rim_slots(table_x))
+    signal_reach(0)
 
     for copy in load_slots:
         copy.wait()
@@ -505,6 +528,8 @@
     load_first.wait()
 
     swap_x.arrive()
+    pl.semaphore_wait(reach.at[0], 2)
+    signal_reach(1)
     clear_outside(table_x)
     share_x = share(1, table_x, other_x)
     convolve(table_x, plan, IN, OUT_CHAIN, first_weight, sums, False)
@@ -518,18 +543,21 @@
         hide(block)
     rim_h = table_h.at[pl.ds(0, RIM)]
     swap_h = Swap(1, send_sems, recv_sems, [rim_h] * 8, rim_slots(table_h))
-    pl.loop(RIM, BLOCKS)(hide)
+    for block in range(RIM, BLOCKS):
+        hide(block)
+    swap_x.finish()
 
     load_other.wait()
     load_second.wait()
     load_grad.wait()
     swap_h.arrive()
+    pl.semaphore_wait(reach.at[1], 2)
+    signal_reach(2)
     clear_outside(table_h)
     share_h = share(2, table_h, other_h)
     convolve(table_h, plan, IN, OUT_CHAIN, second_weight, sums, False)
 
-    @pl.loop(0, BLOCKS)
-    def _(block):
+    for block in range(BLOCKS):
         joined = sums[plan[OUT_LAST, block]] + table_x[block].astype(jnp.float32)
         gate = sigmoid(joined)
         result[block] = (joined * gate).astype(jnp.bfloat16)
@@ -545,8 +573,7 @@
     )
 
     def give(buffer):
-        @pl.loop(0, 8)
-        def _(g):
+        for g in range(8):
             for r in range(RIM):
                 buffer[g, r] = sums[plan[IN_LAST, BLOCKS + RIM * g + r]].astype(jnp.bfloat16)
 
@@ -560,8 +587,8 @@
     def descend(block, total):
         first_delta[block] = (total * slope(first_sum[block])).astype(jnp.bfloat16)
 
-    @pl.loop(RIM, BLOCKS)
-    def _(block):
+    swap_h.finish()
+    for block in range(RIM, BLOCKS):
         descend(block, sums[plan[IN_LAST, block]])
 
     share_inner = share(
@@ -587,32 +614,31 @@
     convolve(first_delta, plan, DELTA, IN_CHAIN, first_weight, sums, True)
     give(give_x)
     back_x = Swap(3, send_sems, recv_sems, eight(give_x), eight(got_x))
+    pl.semaphore_wait(reach.at[2], 2)
     second.start_near()
+    back_h.finish()
 
     def land(block, total):
         input_grad[block] = (total + second_delta[block].astype(jnp.float32)).astype(jnp.bfloat16)
 
-    @pl.loop(RIM, BLOCKS)
-    def _(block):
+    for block in range(RIM, BLOCKS):
         land(block, sums[plan[IN_LAST, block]])
-
     second.start_far()
     first.start_near()
+    second.start_back()
     back_x.arrive()
     for r in range(RIM):
         land(r, routed(sums[plan[IN_LAST, r]], got_x, r))
-    first.start_far()
-    second.start_back()
-    first.start_back()
-    second.start_gather()
-    first.start_gather()
-    second.start_core()
-    first.start_core()
     for copy in to_core:
         copy.wait_send()
-    for swap in (swap_x, swap_h, back_h, back_x):
-        swap.finish()
+    back_x.finish()
+    first.start_far()
+    second.start_gather()
+    first.start_back()
+    second.start_core()
+    first.start_gather()
     second.finish()
+    first.start_core()
     first.finish()
 
 

time: 76 us -> 74.2 us (0.976)
  Pallas kernels: 75.2 us -> 73.5 us
    pallas_call x1, Pallas kernels: 73.9 us -> 72.2 us  [shards(): pl.pallas_call(functools.partial(block_kernel, scale), out_shape=(field,...]
where the time goes in v4:
time: 74.2 us; the launch traced here: 74.1 us
  Pallas kernels  73.5 us (99%)
    pallas_call x1, Pallas kernels, shards(): pl.pallas_call(functools.partial(block_kernel, scale), out_shape=(field,...  72.2 us

profile of v4, /device:TPU:1, one launch (start us, length us, event | category | flops | bytes accessed | tf_op | source)
XLA Modules:
  0.0 74.1 jit_solution(17769886016885852766)
XLA Ops:
  0.6 72.2 %block.1 = (bf16[8,64,128]{2,1,0:T(8,128)(2,1)S(1)}, bf16[8,64,128]{2,1,0:T(8,128)(2,1)S(1)}, bf16[3584,128]{1,0:T(8,128)(2,1)S(1)}, bf16[3584,128]{1,0:T(8,128)(2,1)S(1)}) custom-call(bf16[8,64,128]{2,1,0:T(8,128)(2,1)} %bitcast.17, bf16[27,128,128]{2,1,0:T(8,128)(2,1)} %first_weight_in.1, bf16[27,128,128]{2,1,0:T(8,128)(2,1)} %second_weight_in.1, ...), custom_call_target="tpu_custom_call" | custom-call | flops 679477248 | bytes 3670016 | tf_op jit(solution)/shard_map/block/pallas_call | solution.py:671
  72.8 1.3 %place.1 = (bf16[8,64,128]{2,1,0:T(8,128)(2,1)}, bf16[8,64,128]{2,1,0:T(8,128)(2,1)}, bf16[3456,128]{1,0:T(8,128)(2,1)}, bf16[3456,128]{1,0:T(8,128)(2,1)}) custom-call(bf16[8,64,128]{2,1,0:T(8,128)(2,1)S(1)} %get-tuple-element.12.refs_0_, bf16[8,64,128]{2,1,0:T(8,128)(2,1)S(1)} %get-tuple-element.13.refs_1_, ...), custom_call_target="tpu_custom_call" | custom-call | tf_op jit(solution)/shard_map/place/pallas_call | solution.py:698

commit v5 on v4

--- a/solution.py
+++ b/solution.py
@@ -46,6 +46,10 @@
 PLANE = sorted(range(1, 16), key=lambda d: -hops(d))
 
 
+def ring_of(d):
+    return min(hops(d), 3) - 1
+
+
 def in_plane(d):
     z, x, y, core = place()
     return device(z, lax.rem(x + d // 4, 4), lax.rem(y + d % 4, 4), core)
@@ -74,6 +78,10 @@
 def far(d):
     z, x, y, core = place()
     return device(lax.rem(z + 4 * d, 16), x, y, core)
+
+
+def wait_bytes(ref, sem):
+    pltpu.make_async_copy(ref, ref, sem).wait()
 
 
 class Reduce:
@@ -84,12 +92,8 @@
         pltpu.VMEM((3, QUARTER, 128), jnp.bfloat16),
         pltpu.VMEM((4, QUARTER, 128), jnp.bfloat16),
         pltpu.VMEM((4 * QUARTER, 128), jnp.bfloat16),
-        pltpu.SemaphoreType.DMA((2, 16)),
-        pltpu.SemaphoreType.DMA((2, 4)),
-        pltpu.SemaphoreType.DMA((2, 4)),
-        pltpu.SemaphoreType.DMA((2, 4)),
-        pltpu.SemaphoreType.DMA((2, 16)),
-        pltpu.SemaphoreType.DMA((2, 16)),
+        pltpu.SemaphoreType.DMA((6,)),
+        pltpu.SemaphoreType.DMA((8,)),
     ]
 
     def __init__(self, out, scale, *scratch):
@@ -101,120 +105,101 @@
             self.got_near,
             self.fars,
             self.whole,
-            self.plane_sems,
-            self.near_sems,
-            self.far_sems,
-            self.back_sems,
-            self.gather_sems,
-            self.core_sems,
+            self.send_sems,
+            self.recv_sems,
         ) = scratch
-        self.sent = []
 
     def clear(self):
         self.plane_sum[PIECE:] = jnp.zeros((4 * QUARTER - PIECE, 128), jnp.bfloat16)
 
-    def send(self, src, dst, sems, index, device_id):
-        copy = pltpu.make_async_remote_copy(
+    def send(self, src, dst, send_index, recv_index, device_id):
+        pltpu.make_async_remote_copy(
             src_ref=src,
             dst_ref=dst,
-            send_sem=sems.at[0, index],
-            recv_sem=sems.at[1, index],
+            send_sem=self.send_sems.at[send_index],
+            recv_sem=self.recv_sems.at[recv_index],
             device_id=device_id,
             device_id_type=MESH,
-        )
-        copy.start()
-        self.sent.append(copy)
-
-    def drain(self):
-        for copy in self.sent:
-            copy.wait_send()
-        self.sent = []
-
-    def arrive(self, dst, sems, index):
-        pltpu.make_async_copy(dst, dst, sems.at[1, index]).wait()
+        ).start()
+
+    def sent(self, index, count, size):
+        wait_bytes(self.part.at[pl.ds(0, count * size)], self.send_sems.at[index])
 
     def start_plane(self):
         for d in PLANE:
             self.send(
                 self.part.at[rows(plane_index(d) * PIECE, PIECE)],
                 self.got_plane.at[d - 1],
-                self.plane_sems,
-                d,
+                0,
+                0,
                 in_plane(d),
             )
 
     def start_near(self):
+        wait_bytes(self.got_plane, self.recv_sems.at[0])
         total = self.part[rows(plane_index(0) * PIECE, PIECE)].astype(jnp.float32)
-        for d in reversed(PLANE):
-            self.arrive(self.got_plane.at[d - 1], self.plane_sems, d)
-            total = total + self.got_plane[d - 1].astype(jnp.float32)
+        for d in range(15):
+            total = total + self.got_plane[d].astype(jnp.float32)
         self.plane_sum[:PIECE] = total.astype(jnp.bfloat16)
-        before, self.sent = self.sent, []
         for d in (2, 1, 3):
             index, target = near(d)
             self.send(
                 self.plane_sum.at[rows(index * QUARTER, QUARTER)],
                 self.got_near.at[d - 1],
-                self.near_sems,
-                d,
+                1,
+                1,
                 target,
             )
-        for copy in before:
-            copy.wait_send()
+        self.sent(0, 15, PIECE)
 
     def start_far(self):
         index, _ = near(0)
+        wait_bytes(self.got_near, self.recv_sems.at[1])
         total = self.plane_sum[rows(index * QUARTER, QUARTER)].astype(jnp.float32)
-        for d in (1, 2, 3):
-            self.arrive(self.got_near.at[d - 1], self.near_sems, d)
-            total = total + self.got_near[d - 1].astype(jnp.float32)
+        for d in range(3):
+            total = total + self.got_near[d].astype(jnp.float32)
         group = place()[0] // 4
         self.fars[group] = total.astype(jnp.bfloat16)
         for d in (2, 1, 3):
-            self.send(self.fars.at[group], self.fars.at[group], self.far_sems, d, far(d))
+            self.send(self.fars.at[group], self.fars.at[group], 2, 2, far(d))
+        self.sent(1, 3, QUARTER)
 
     def start_back(self):
-        group = place()[0] // 4
-        for d in (1, 3, 2):
-            self.arrive(self.fars.at[lax.rem(group + 4 - d, 4)], self.far_sems, d)
+        wait_bytes(self.fars.at[pl.ds(0, 3)], self.recv_sems.at[2])
         total = self.fars[0].astype(jnp.float32)
         for other in (1, 2, 3):
             total = total + self.fars[other].astype(jnp.float32)
-        index, _ = near(0)
-        piece = rows(index * QUARTER, QUARTER)
+        piece = rows(near(0)[0] * QUARTER, QUARTER)
         self.whole[piece] = (total * self.scale).astype(jnp.bfloat16)
         for d in (2, 1, 3):
-            self.send(self.whole.at[piece], self.whole.at[piece], self.back_sems, d, near(d)[1])
+            self.send(self.whole.at[piece], self.whole.at[piece], 3, 3, near(d)[1])
+        self.sent(2, 3, QUARTER)
 
     def spot(self, d, core):
         return self.out.at[rows(core * HALF + plane_index(d) * PIECE, PIECE)]
 
     def start_gather(self):
-        for d in (1, 3, 2):
-            piece = self.whole.at[rows(near(4 - d)[0] * QUARTER, QUARTER)]
-            self.arrive(piece, self.back_sems, d)
-        core = place()[3]
-        own = self.spot(0, core)
+        wait_bytes(self.whole.at[pl.ds(0, 3 * QUARTER)], self.recv_sems.at[3])
+        own = self.spot(0, place()[3])
         own[...] = self.whole[:PIECE]
-        before, self.sent = self.sent, []
         for d in PLANE:
-            self.send(own, own, self.gather_sems, d, in_plane(d))
-        self.send(own, own, self.core_sems, 0, partner())
-        for copy in before:
-            copy.wait_send()
+            self.send(own, own, 4, 4 + ring_of(d), in_plane(d))
+        self.send(own, own, 5, 7, partner())
+        self.sent(3, 3, QUARTER)
 
     def start_core(self):
         core = place()[3]
-        for d in reversed(PLANE):
-            piece = self.spot(opposite(d), core)
-            self.arrive(piece, self.gather_sems, d)
-            self.send(piece, piece, self.core_sems, d, partner())
+        for index in range(3):
+            group = [d for d in PLANE if ring_of(d) == index]
+            wait_bytes(self.part.at[pl.ds(0, len(group) * PIECE)], self.recv_sems.at[4 + index])
+            for d in group:
+                piece = self.spot(opposite(d), core)
+                self.send(piece, piece, 5, 7, partner())
+        self.sent(4, 15, PIECE)
 
     def finish(self):
-        core = place()[3]
-        for d in range(16):
-            self.arrive(self.spot(opposite(d), 1 - core), self.core_sems, d)
-        self.drain()
+        wait_bytes(self.part, self.recv_sems.at[7])
+        self.sent(5, 16, PIECE)
 
 
 def enter(peers):
@@ -286,7 +271,7 @@
     chain(jnp.where(live > 0, source, -1), IN_CHAIN, IN_LAST)
 
 
-UNROLL = 9
+UNROLL = 27
 
 
 def step_loop(count, body, unroll=None):
@@ -334,31 +319,31 @@
         )
         part[rows(j * 128, 128)] = product.astype(jnp.bfloat16)
 
-    step_loop(HALF_OFFSETS, body, 7)
+    step_loop(HALF_OFFSETS, body, 14)
 
 
 class Swap:
-    def __init__(self, index, send_sems, recv_sems, sources, targets):
-        self.copies = []
+    def __init__(self, index, sems, sources, targets, blocks):
+        self.sems, self.blocks = [sems.at[side, index] for side in (0, 1)], blocks
         for g, direction in enumerate(DIRECTIONS):
-            copy = pltpu.make_async_remote_copy(
+            pltpu.make_async_remote_copy(
                 src_ref=sources[g],
                 dst_ref=targets[7 - g],
-                send_sem=send_sems.at[index, g],
-                recv_sem=recv_sems.at[index, 7 - g],
+                send_sem=self.sems[0],
+                recv_sem=self.sems[1],
                 device_id=neighbour(direction),
                 device_id_type=MESH,
-            )
-            copy.start()
-            self.copies.append(copy)
+            ).start()
 
     def arrive(self):
-        for copy in self.copies:
-            copy.wait_recv()
+        wait_bytes(self.blocks, self.sems[1])
 
     def finish(self):
-        for copy in self.copies:
-            copy.wait_send()
+        wait_bytes(self.blocks, self.sems[0])
+
+
+def beyond(table):
+    return table.at[pl.ds(BLOCKS, 8 * RIM)]
 
 
 def rim_slots(table):
@@ -384,9 +369,7 @@
 
 BLOCK_SET = (VOXELS, 128)
 SCRATCH = [
-    pltpu.VMEM((2, OFFSETS), jnp.int32),
-    pltpu.VMEM((2, OFFSETS), jnp.int32),
-    pltpu.VMEM((2, OFFSETS), jnp.int32),
+    pltpu.VMEM((3, 2, OFFSETS), jnp.int32),
     pltpu.VMEM((OFFSETS, 128, 128), jnp.bfloat16),
     pltpu.VMEM((OFFSETS, 128, 128), jnp.bfloat16),
     pltpu.VMEM((BLOCKS,) + BLOCK_SET, jnp.bfloat16),
@@ -408,10 +391,9 @@
     pltpu.VMEM((8, RIM) + BLOCK_SET, jnp.bfloat16),
     pltpu.VMEM((8, RIM) + BLOCK_SET, jnp.bfloat16),
     pltpu.VMEM((8, RIM) + BLOCK_SET, jnp.bfloat16),
-    pltpu.SemaphoreType.DMA((9,)),
-    pltpu.SemaphoreType.DMA((2, 8)),
-    pltpu.SemaphoreType.DMA((4, 8)),
-    pltpu.SemaphoreType.DMA((4, 8)),
+    pltpu.SemaphoreType.DMA((5,)),
+    pltpu.SemaphoreType.DMA((7,)),
+    pltpu.SemaphoreType.DMA((2, 4)),
     pltpu.SemaphoreType.REGULAR((3,)),
 ]
 
@@ -432,9 +414,7 @@
     *scratch,
 ):
     (
-        in_rows,
-        out_rows,
-        live_rows,
+        slot_rows,
         first_weight,
         second_weight,
         out_grad,
@@ -458,15 +438,13 @@
         got_x,
         load_sems,
         core_sems,
-        send_sems,
-        recv_sems,
+        swap_sems,
         reach,
     ) = scratch[: len(SCRATCH)]
     count = len(Reduce.scratch)
     reduces = scratch[len(SCRATCH) :]
     first = Reduce(first_grad, scale, *reduces[:count])
     second = Reduce(second_grad, scale, *reduces[count:])
-    to_core = []
 
     def load(index, src, dst):
         copy = pltpu.make_async_copy(src, dst, load_sems.at[index])
@@ -477,25 +455,21 @@
         copy = pltpu.make_async_remote_copy(
             src_ref=src,
             dst_ref=dst,
-            send_sem=core_sems.at[0, index],
-            recv_sem=core_sems.at[1, index],
+            send_sem=core_sems.at[6],
+            recv_sem=core_sems.at[index],
             device_id=partner(),
             device_id_type=MESH,
         )
         copy.start()
-        to_core.append(copy)
         return copy
 
     own = table_x.at[pl.ds(0, BLOCKS)]
     load_x = load(0, voxels_in, own)
-    load_slots = [
-        load(1, in_slots, in_rows),
-        load(2, out_slots, out_rows),
-        load(3, live_slots, live_rows),
-    ]
-    load_first = load(4, first_weight_in, first_weight)
-    load_second = load(5, second_weight_in, second_weight)
-    load_grad = load(6, out_grad_in, out_grad)
+    for index, slots in enumerate((in_slots, out_slots, live_slots)):
+        load(1, slots, slot_rows.at[index])
+    load_first = load(2, first_weight_in, first_weight)
+    load_second = load(3, second_weight_in, second_weight)
+    load_grad = load(4, out_grad_in, out_grad)
 
     def signal_reach(step):
         for d in (1 << step, -(1 << step)):
@@ -508,13 +482,12 @@
     )
     load_x.wait()
     rim_x = table_x.at[pl.ds(0, RIM)]
-    swap_x = Swap(0, send_sems, recv_sems, [rim_x] * 8, rim_slots(table_x))
+    swap_x = Swap(0, swap_sems, [rim_x] * 8, rim_slots(table_x), beyond(table_x))
     signal_reach(0)
 
-    for copy in load_slots:
-        copy.wait()
-    write_plan(in_rows, out_rows, live_rows, plan_rows)
-    load_plan = load(7, plan_rows, plan)
+    wait_bytes(slot_rows, load_sems.at[1])
+    write_plan(slot_rows.at[0], slot_rows.at[1], slot_rows.at[2], plan_rows)
+    load_plan = load(0, plan_rows, plan)
     share_plan = share(0, plan_rows, other_rows)
     zeros = jnp.zeros(BLOCK_SET, jnp.bfloat16)
     for delta in (first_delta, second_delta, other_first, other_second):
@@ -524,13 +497,14 @@
     second.clear()
     load_plan.wait()
     share_plan.wait_recv()
-    load_other = load(8, other_rows, other_plan)
+    load_other = load(1, other_rows, other_plan)
     load_first.wait()
 
     swap_x.arrive()
     pl.semaphore_wait(reach.at[0], 2)
     signal_reach(1)
     clear_outside(table_x)
+    share_plan.wait_send()
     share_x = share(1, table_x, other_x)
     convolve(table_x, plan, IN, OUT_CHAIN, first_weight, sums, False)
 
@@ -542,7 +516,7 @@
     for block in range(RIM):
         hide(block)
     rim_h = table_h.at[pl.ds(0, RIM)]
-    swap_h = Swap(1, send_sems, recv_sems, [rim_h] * 8, rim_slots(table_h))
+    swap_h = Swap(1, swap_sems, [rim_h] * 8, rim_slots(table_h), beyond(table_h))
     for block in range(RIM, BLOCKS):
         hide(block)
     swap_x.finish()
@@ -554,6 +528,7 @@
     pl.semaphore_wait(reach.at[1], 2)
     signal_reach(2)
     clear_outside(table_h)
+    share_x.wait_send()
     share_h = share(2, table_h, other_h)
     convolve(table_h, plan, IN, OUT_CHAIN, second_weight, sums, False)
 
@@ -568,6 +543,7 @@
     def all_of(delta, first_block, last_block):
         return delta.at[pl.ds(first_block, last_block - first_block)]
 
+    share_h.wait_send()
     share_second = share(
         3, all_of(second_delta, 0, BLOCKS), all_of(other_second, 0, BLOCKS)
     )
@@ -582,7 +558,7 @@
 
     convolve(second_delta, plan, DELTA, IN_CHAIN, second_weight, sums, True)
     give(give_h)
-    back_h = Swap(2, send_sems, recv_sems, eight(give_h), eight(got_h))
+    back_h = Swap(2, swap_sems, eight(give_h), eight(got_h), got_h)
 
     def descend(block, total):
         first_delta[block] = (total * slope(first_sum[block])).astype(jnp.bfloat16)
@@ -591,6 +567,7 @@
     for block in range(RIM, BLOCKS):
         descend(block, sums[plan[IN_LAST, block]])
 
+    share_second.wait_send()
     share_inner = share(
         4, all_of(first_delta, RIM, BLOCKS), all_of(other_first, RIM, BLOCKS)
     )
@@ -604,6 +581,7 @@
     back_h.arrive()
     for r in range(RIM):
         descend(r, routed(sums[plan[IN_LAST, r]], got_h, r))
+    share_inner.wait_send()
     share_rim = share(5, all_of(first_delta, 0, RIM), all_of(other_first, 0, RIM))
     share_x.wait_recv()
     share_inner.wait_recv()
@@ -613,7 +591,7 @@
 
     convolve(first_delta, plan, DELTA, IN_CHAIN, first_weight, sums, True)
     give(give_x)
-    back_x = Swap(3, send_sems, recv_sems, eight(give_x), eight(got_x))
+    back_x = Swap(3, swap_sems, eight(give_x), eight(got_x), got_x)
     pl.semaphore_wait(reach.at[2], 2)
     second.start_near()
     back_h.finish()
@@ -629,8 +607,7 @@
     back_x.arrive()
     for r in range(RIM):
         land(r, routed(sums[plan[IN_LAST, r]], got_x, r))
-    for copy in to_core:
-        copy.wait_send()
+    share_rim.wait_send()
     back_x.finish()
     first.start_far()
     second.start_gather()

time: 74.2 us -> 71.5 us (0.964)
  Pallas kernels: 73.5 us -> 70.8 us
    pallas_call x1, Pallas kernels: 72.2 us -> 69.5 us  [shards(): pl.pallas_call(functools.partial(block_kernel, scale), out_shape=(field,...]
where the time goes in v5:
time: 71.5 us; the launch traced here: 71.4 us
  Pallas kernels  70.8 us (99%)
    pallas_call x1, Pallas kernels, shards(): pl.pallas_call(functools.partial(block_kernel, scale), out_shape=(field,...  69.5 us

profile of v5, /device:TPU:1, one launch (start us, length us, event | category | flops | bytes accessed | tf_op | source)
XLA Modules:
  0.0 71.4 jit_solution(16529677676010522318)
XLA Ops:
  0.6 69.5 %block.1 = (bf16[8,64,128]{2,1,0:T(8,128)(2,1)S(1)}, bf16[8,64,128]{2,1,0:T(8,128)(2,1)S(1)}, bf16[3584,128]{1,0:T(8,128)(2,1)S(1)}, bf16[3584,128]{1,0:T(8,128)(2,1)S(1)}) custom-call(bf16[8,64,128]{2,1,0:T(8,128)(2,1)} %bitcast.17, bf16[27,128,128]{2,1,0:T(8,128)(2,1)} %first_weight_in.1, bf16[27,128,128]{2,1,0:T(8,128)(2,1)} %second_weight_in.1, ...), custom_call_target="tpu_custom_call" | custom-call | flops 679477248 | bytes 3670016 | tf_op jit(solution)/shard_map/block/pallas_call | solution.py:648
  70.1 1.3 %place.1 = (bf16[8,64,128]{2,1,0:T(8,128)(2,1)}, bf16[8,64,128]{2,1,0:T(8,128)(2,1)}, bf16[3456,128]{1,0:T(8,128)(2,1)}, bf16[3456,128]{1,0:T(8,128)(2,1)}) custom-call(bf16[8,64,128]{2,1,0:T(8,128)(2,1)S(1)} %get-tuple-element.12.refs_0_, bf16[8,64,128]{2,1,0:T(8,128)(2,1)S(1)} %get-tuple-element.13.refs_1_, ...), custom_call_target="tpu_custom_call" | custom-call | tf_op jit(solution)/shard_map/place/pallas_call | solution.py:675

commit v6 on v5

--- a/solution.py
+++ b/solution.py
@@ -16,7 +16,6 @@
 FULL = 2 * HALF
 HALF_OFFSETS = HALF // 128
 PIECE = HALF // 16
-QUARTER = 32
 
 
 def rows(start, size):
@@ -47,7 +46,7 @@
 
 
 def ring_of(d):
-    return min(hops(d), 3) - 1
+    return hops(d) - 1
 
 
 def in_plane(d):
@@ -64,20 +63,12 @@
     return (4 - d // 4) % 4 * 4 + (4 - d % 4) % 4
 
 
-def near(d):
-    z, x, y, core = place()
-    index = lax.rem(z + d, 4)
-    return index, device(z // 4 * 4 + index, x, y, core)
-
-
 def ring(d):
     z, x, y, core = place()
     return device(lax.rem(z + d + 16, 16), x, y, core)
 
 
-def far(d):
-    z, x, y, core = place()
-    return device(lax.rem(z + 4 * d, 16), x, y, core)
+SPREAD = [1, 2, 3, 4, 15, 5, 14, 6, 13, 7, 12, 8, 11, 10, 9]
 
 
 def wait_bytes(ref, sem):
@@ -88,11 +79,9 @@
     scratch = [
         pltpu.VMEM((HALF, 128), jnp.bfloat16),
         pltpu.VMEM((15, PIECE, 128), jnp.bfloat16),
-        pltpu.VMEM((4 * QUARTER, 128), jnp.bfloat16),
-        pltpu.VMEM((3, QUARTER, 128), jnp.bfloat16),
-        pltpu.VMEM((4, QUARTER, 128), jnp.bfloat16),
-        pltpu.VMEM((4 * QUARTER, 128), jnp.bfloat16),
-        pltpu.SemaphoreType.DMA((6,)),
+        pltpu.VMEM((PIECE, 128), jnp.bfloat16),
+        pltpu.VMEM((15, PIECE, 128), jnp.bfloat16),
+        pltpu.SemaphoreType.DMA((5,)),
         pltpu.SemaphoreType.DMA((8,)),
     ]
 
@@ -102,15 +91,10 @@
             self.part,
             self.got_plane,
             self.plane_sum,
-            self.got_near,
-            self.fars,
-            self.whole,
+            self.got_root,
             self.send_sems,
             self.recv_sems,
         ) = scratch
-
-    def clear(self):
-        self.plane_sum[PIECE:] = jnp.zeros((4 * QUARTER - PIECE, 128), jnp.bfloat16)
 
     def send(self, src, dst, send_index, recv_index, device_id):
         pltpu.make_async_remote_copy(
@@ -135,71 +119,71 @@
                 in_plane(d),
             )
 
-    def start_near(self):
+    def start_root(self):
         wait_bytes(self.got_plane, self.recv_sems.at[0])
         total = self.part[rows(plane_index(0) * PIECE, PIECE)].astype(jnp.float32)
         for d in range(15):
             total = total + self.got_plane[d].astype(jnp.float32)
-        self.plane_sum[:PIECE] = total.astype(jnp.bfloat16)
-        for d in (2, 1, 3):
-            index, target = near(d)
-            self.send(
-                self.plane_sum.at[rows(index * QUARTER, QUARTER)],
-                self.got_near.at[d - 1],
-                1,
-                1,
-                target,
-            )
+        self.plane_sum[...] = total.astype(jnp.bfloat16)
+        z, x, y, core = place()
+
+        @pl.when(z > 0)
+        def _():
+            self.send(self.plane_sum, self.got_root.at[z - 1], 1, 1, device(0, x, y, core))
+
         self.sent(0, 15, PIECE)
-
-    def start_far(self):
-        index, _ = near(0)
-        wait_bytes(self.got_near, self.recv_sems.at[1])
-        total = self.plane_sum[rows(index * QUARTER, QUARTER)].astype(jnp.float32)
-        for d in range(3):
-            total = total + self.got_near[d].astype(jnp.float32)
-        group = place()[0] // 4
-        self.fars[group] = total.astype(jnp.bfloat16)
-        for d in (2, 1, 3):
-            self.send(self.fars.at[group], self.fars.at[group], 2, 2, far(d))
-        self.sent(1, 3, QUARTER)
-
-    def start_back(self):
-        wait_bytes(self.fars.at[pl.ds(0, 3)], self.recv_sems.at[2])
-        total = self.fars[0].astype(jnp.float32)
-        for other in (1, 2, 3):
-            total = total + self.fars[other].astype(jnp.float32)
-        piece = rows(near(0)[0] * QUARTER, QUARTER)
-        self.whole[piece] = (total * self.scale).astype(jnp.bfloat16)
-        for d in (2, 1, 3):
-            self.send(self.whole.at[piece], self.whole.at[piece], 3, 3, near(d)[1])
-        self.sent(2, 3, QUARTER)
 
     def spot(self, d, core):
         return self.out.at[rows(core * HALF + plane_index(d) * PIECE, PIECE)]
 
-    def start_gather(self):
-        wait_bytes(self.whole.at[pl.ds(0, 3 * QUARTER)], self.recv_sems.at[3])
-        own = self.spot(0, place()[3])
-        own[...] = self.whole[:PIECE]
+    def start_spread(self):
+        z, x, y, core = place()
+        own = self.spot(0, core)
+
+        def spread(planes):
+            for plane in planes:
+                self.send(own, own, 2, 2, device(plane, x, y, core))
+
+        @pl.when(z == 0)
+        def _():
+            wait_bytes(self.got_root, self.recv_sems.at[1])
+            total = self.plane_sum[...].astype(jnp.float32)
+            for plane in range(15):
+                total = total + self.got_root[plane].astype(jnp.float32)
+            own[...] = (total * self.scale).astype(jnp.bfloat16)
+            spread(SPREAD[:4])
+
+        @pl.when(z > 0)
+        def _():
+            self.sent(1, 1, PIECE)
+            wait_bytes(own, self.recv_sems.at[2])
+
         for d in PLANE:
-            self.send(own, own, 4, 4 + ring_of(d), in_plane(d))
-        self.send(own, own, 5, 7, partner())
-        self.sent(3, 3, QUARTER)
+            self.send(own, own, 3, 3 + ring_of(d), in_plane(d))
+        self.send(own, own, 4, 7, partner())
+
+        @pl.when(z == 0)
+        def _():
+            spread(SPREAD[4:])
 
     def start_core(self):
         core = place()[3]
-        for index in range(3):
+        for index in range(4):
             group = [d for d in PLANE if ring_of(d) == index]
-            wait_bytes(self.part.at[pl.ds(0, len(group) * PIECE)], self.recv_sems.at[4 + index])
+            wait_bytes(self.part.at[pl.ds(0, len(group) * PIECE)], self.recv_sems.at[3 + index])
             for d in group:
                 piece = self.spot(opposite(d), core)
-                self.send(piece, piece, 5, 7, partner())
-        self.sent(4, 15, PIECE)
+                self.send(piece, piece, 4, 7, partner())
+
+        @pl.when(place()[0] == 0)
+        def _():
+            self.sent(2, 15, PIECE)
+
+        self.sent(3, 15, PIECE)
 
     def finish(self):
         wait_bytes(self.part, self.recv_sems.at[7])
-        self.sent(5, 16, PIECE)
+        self.sent(4, 16, PIECE)
 
 
 def enter(peers):
@@ -493,8 +477,6 @@
     for delta in (first_delta, second_delta, other_first, other_second):
         delta[BLOCKS] = zeros
     sums[0] = jnp.zeros(BLOCK_SET, jnp.float32)
-    first.clear()
-    second.clear()
     load_plan.wait()
     share_plan.wait_recv()
     load_other = load(1, other_rows, other_plan)
@@ -578,6 +560,7 @@
     )
     second.start_plane()
 
+    pl.semaphore_wait(reach.at[2], 2)
     back_h.arrive()
     for r in range(RIM):
         descend(r, routed(sums[plan[IN_LAST, r]], got_h, r))
@@ -589,11 +572,10 @@
     weight_terms((table_x, other_x), (first_delta, other_first), (plan, other_plan), first.part)
     first.start_plane()
 
+    second.start_root()
     convolve(first_delta, plan, DELTA, IN_CHAIN, first_weight, sums, True)
     give(give_x)
     back_x = Swap(3, swap_sems, eight(give_x), eight(got_x), got_x)
-    pl.semaphore_wait(reach.at[2], 2)
-    second.start_near()
     back_h.finish()
 
     def land(block, total):
@@ -601,19 +583,15 @@
 
     for block in range(RIM, BLOCKS):
         land(block, sums[plan[IN_LAST, block]])
-    second.start_far()
-    first.start_near()
-    second.start_back()
+    first.start_root()
     back_x.arrive()
     for r in range(RIM):
         land(r, routed(sums[plan[IN_LAST, r]], got_x, r))
     share_rim.wait_send()
     back_x.finish()
-    first.start_far()
-    second.start_gather()
-    first.start_back()
+    second.start_spread()
     second.start_core()
-    first.start_gather()
+    first.start_spread()
     second.finish()
     first.start_core()
     first.finish()

time: 71.5 us -> 67.9 us (0.950); the launches traced: 71.4 us -> 66.6 us
  Pallas kernels: 70.8 us -> 66 us
    pallas_call x1, Pallas kernels: 69.5 us -> 64.6 us  [shards(): pl.pallas_call(functools.partial(block_kernel, scale), out_shape=(field,...]
where the time goes in v6:
time: 67.9 us; the launch traced here: 66.6 us
  Pallas kernels  66 us (97%)
    pallas_call x1, Pallas kernels, shards(): pl.pallas_call(functools.partial(block_kernel, scale), out_shape=(field,...  64.6 us

profile of v6, /device:TPU:1, one launch (start us, length us, event | category | flops | bytes accessed | tf_op | source)
XLA Modules:
  0.0 66.6 jit_solution(3245386194290482896)
XLA Ops:
  0.6 64.6 %block.1 = (bf16[8,64,128]{2,1,0:T(8,128)(2,1)S(1)}, bf16[8,64,128]{2,1,0:T(8,128)(2,1)S(1)}, bf16[3584,128]{1,0:T(8,128)(2,1)S(1)}, bf16[3584,128]{1,0:T(8,128)(2,1)S(1)}) custom-call(bf16[8,64,128]{2,1,0:T(8,128)(2,1)} %bitcast.17, bf16[27,128,128]{2,1,0:T(8,128)(2,1)} %first_weight_in.1, bf16[27,128,128]{2,1,0:T(8,128)(2,1)} %second_weight_in.1, ...), custom_call_target="tpu_custom_call" | custom-call | flops 679477248 | bytes 3670016 | tf_op jit(solution)/shard_map/block/pallas_call | solution.py:626
  65.3 1.3 %place.1 = (bf16[8,64,128]{2,1,0:T(8,128)(2,1)}, bf16[8,64,128]{2,1,0:T(8,128)(2,1)}, bf16[3456,128]{1,0:T(8,128)(2,1)}, bf16[3456,128]{1,0:T(8,128)(2,1)}) custom-call(bf16[8,64,128]{2,1,0:T(8,128)(2,1)S(1)} %get-tuple-element.12.refs_0_, bf16[8,64,128]{2,1,0:T(8,128)(2,1)S(1)} %get-tuple-element.13.refs_1_, ...), custom_call_target="tpu_custom_call" | custom-call | tf_op jit(solution)/shard_map/place/pallas_call | solution.py:653

commit v7 on v6

--- a/solution.py
+++ b/solution.py
@@ -486,8 +486,6 @@
     pl.semaphore_wait(reach.at[0], 2)
     signal_reach(1)
     clear_outside(table_x)
-    share_plan.wait_send()
-    share_x = share(1, table_x, other_x)
     convolve(table_x, plan, IN, OUT_CHAIN, first_weight, sums, False)
 
     def hide(block):
@@ -501,6 +499,8 @@
     swap_h = Swap(1, swap_sems, [rim_h] * 8, rim_slots(table_h), beyond(table_h))
     for block in range(RIM, BLOCKS):
         hide(block)
+    share_plan.wait_send()
+    share_x = share(1, table_x, other_x)
     swap_x.finish()
 
     load_other.wait()
@@ -573,25 +573,25 @@
     first.start_plane()
 
     second.start_root()
+    back_h.finish()
+
+    def land(block, total):
+        input_grad[block] = (total + second_delta[block].astype(jnp.float32)).astype(jnp.bfloat16)
+
+    first.start_root()
     convolve(first_delta, plan, DELTA, IN_CHAIN, first_weight, sums, True)
     give(give_x)
     back_x = Swap(3, swap_sems, eight(give_x), eight(got_x), got_x)
-    back_h.finish()
-
-    def land(block, total):
-        input_grad[block] = (total + second_delta[block].astype(jnp.float32)).astype(jnp.bfloat16)
-
     for block in range(RIM, BLOCKS):
         land(block, sums[plan[IN_LAST, block]])
-    first.start_root()
+    second.start_spread()
     back_x.arrive()
     for r in range(RIM):
         land(r, routed(sums[plan[IN_LAST, r]], got_x, r))
     share_rim.wait_send()
     back_x.finish()
-    second.start_spread()
+    first.start_spread()
     second.start_core()
-    first.start_spread()
     second.finish()
     first.start_core()
     first.finish()

time: 67.9 us -> 65.8 us (0.969)
  the two profiles are of different devices: /device:TPU:1 before, /device:TPU:257 now
where the time goes in v7:
time: 65.8 us; the launch traced here: 65.7 us
  Pallas kernels  65.1 us (99%)
    pallas_call x1, Pallas kernels, shards(): pl.pallas_call(functools.partial(block_kernel, scale), out_shape=(field,...  63.8 us
    pallas_call x1, Pallas kernels, shards(): pl.pallas_call(lambda *refs: place_kernel(refs[0], refs[1], refs[2].at[pl...  1.33 us

profile of v7, /device:TPU:257, one launch (start us, length us, event | category | flops | bytes accessed | tf_op | source)
XLA Modules:
  0.0 65.7 jit_solution(11381391181423225339)
XLA Ops:
  0.6 63.8 %block.1 = (bf16[8,64,128]{2,1,0:T(8,128)(2,1)S(1)}, bf16[8,64,128]{2,1,0:T(8,128)(2,1)S(1)}, bf16[3584,128]{1,0:T(8,128)(2,1)S(1)}, bf16[3584,128]{1,0:T(8,128)(2,1)S(1)}) custom-call(bf16[8,64,128]{2,1,0:T(8,128)(2,1)} %bitcast.17, bf16[27,128,128]{2,1,0:T(8,128)(2,1)} %first_weight_in.1, bf16[27,128,128]{2,1,0:T(8,128)(2,1)} %second_weight_in.1, ...), custom_call_target="tpu_custom_call" | custom-call | flops 679477248 | bytes 3670016 | tf_op jit(solution)/shard_map/block/pallas_call | solution.py:626
  64.4 1.3 %place.1 = (bf16[8,64,128]{2,1,0:T(8,128)(2,1)}, bf16[8,64,128]{2,1,0:T(8,128)(2,1)}, bf16[3456,128]{1,0:T(8,128)(2,1)}, bf16[3456,128]{1,0:T(8,128)(2,1)}) custom-call(bf16[8,64,128]{2,1,0:T(8,128)(2,1)S(1)} %get-tuple-element.12.refs_0_, bf16[8,64,128]{2,1,0:T(8,128)(2,1)S(1)} %get-tuple-element.13.refs_1_, ...), custom_call_target="tpu_custom_call" | custom-call | tf_op jit(solution)/shard_map/place/pallas_call | solution.py:653

commit v8 on v7

--- a/solution.py
+++ b/solution.py
@@ -186,11 +186,11 @@
         self.sent(4, 16, PIECE)
 
 
-def enter(peers):
+def greet(peers):
     barrier = pltpu.get_barrier_semaphore()
     for peer in peers:
         pl.semaphore_signal(barrier, inc=1, device_id=peer, device_id_type=MESH)
-    pl.semaphore_wait(barrier, len(peers))
+    return lambda: pl.semaphore_wait(barrier, len(peers))
 
 
 BLOCKS, VOXELS, OFFSETS, SLOTS, TABLE = 8, 64, 27, 54, 24
@@ -309,15 +309,22 @@
 class Swap:
     def __init__(self, index, sems, sources, targets, blocks):
         self.sems, self.blocks = [sems.at[side, index] for side in (0, 1)], blocks
-        for g, direction in enumerate(DIRECTIONS):
-            pltpu.make_async_remote_copy(
-                src_ref=sources[g],
-                dst_ref=targets[7 - g],
-                send_sem=self.sems[0],
-                recv_sem=self.sems[1],
-                device_id=neighbour(direction),
-                device_id_type=MESH,
-            ).start()
+        outer = 2 * place()[3] - 1
+        for side in (1, 0, -1):
+            for b in (-1, 1, 0):
+                if (side, b) == (0, 0):
+                    continue
+                a = side * outer
+                cell = 3 * (a + 1) + b + 1
+                g = cell - jnp.where(cell > 4, 1, 0)
+                pltpu.make_async_remote_copy(
+                    src_ref=sources(g),
+                    dst_ref=targets(7 - g),
+                    send_sem=self.sems[0],
+                    recv_sem=self.sems[1],
+                    device_id=neighbour((a, b)),
+                    device_id_type=MESH,
+                ).start()
 
     def arrive(self):
         wait_bytes(self.blocks, self.sems[1])
@@ -331,7 +338,7 @@
 
 
 def rim_slots(table):
-    return [table.at[pl.ds(BLOCKS + RIM * g, RIM)] for g in range(8)]
+    return lambda g: table.at[pl.ds(BLOCKS + RIM * g, RIM)]
 
 
 def clear_outside(table):
@@ -447,6 +454,11 @@
         copy.start()
         return copy
 
+    enter = greet(
+        [neighbour(direction) for direction in DIRECTIONS]
+        + [in_plane(d) for d in PLANE]
+        + [ring(1), ring(-1), partner()]
+    )
     own = table_x.at[pl.ds(0, BLOCKS)]
     load_x = load(0, voxels_in, own)
     for index, slots in enumerate((in_slots, out_slots, live_slots)):
@@ -459,14 +471,10 @@
         for d in (1 << step, -(1 << step)):
             pl.semaphore_signal(reach.at[step], inc=1, device_id=ring(d), device_id_type=MESH)
 
-    enter(
-        [neighbour(direction) for direction in DIRECTIONS]
-        + [in_plane(d) for d in PLANE]
-        + [ring(1), ring(-1), partner()]
-    )
+    enter()
     load_x.wait()
     rim_x = table_x.at[pl.ds(0, RIM)]
-    swap_x = Swap(0, swap_sems, [rim_x] * 8, rim_slots(table_x), beyond(table_x))
+    swap_x = Swap(0, swap_sems, lambda g: rim_x, rim_slots(table_x), beyond(table_x))
     signal_reach(0)
 
     wait_bytes(slot_rows, load_sems.at[1])
@@ -496,7 +504,7 @@
     for block in range(RIM):
         hide(block)
     rim_h = table_h.at[pl.ds(0, RIM)]
-    swap_h = Swap(1, swap_sems, [rim_h] * 8, rim_slots(table_h), beyond(table_h))
+    swap_h = Swap(1, swap_sems, lambda g: rim_h, rim_slots(table_h), beyond(table_h))
     for block in range(RIM, BLOCKS):
         hide(block)
     share_plan.wait_send()
@@ -536,7 +544,7 @@
                 buffer[g, r] = sums[plan[IN_LAST, BLOCKS + RIM * g + r]].astype(jnp.bfloat16)
 
     def eight(buffer):
-        return [buffer.at[g] for g in range(8)]
+        return lambda g: buffer.at[g]
 
     convolve(second_delta, plan, DELTA, IN_CHAIN, second_weight, sums, True)
     give(give_h)
@@ -545,20 +553,20 @@
     def descend(block, total):
         first_delta[block] = (total * slope(first_sum[block])).astype(jnp.bfloat16)
 
-    swap_h.finish()
-    for block in range(RIM, BLOCKS):
-        descend(block, sums[plan[IN_LAST, block]])
-
-    share_second.wait_send()
-    share_inner = share(
-        4, all_of(first_delta, RIM, BLOCKS), all_of(other_first, RIM, BLOCKS)
-    )
     share_h.wait_recv()
     share_second.wait_recv()
     weight_terms(
         (table_h, other_h), (second_delta, other_second), (plan, other_plan), second.part
     )
     second.start_plane()
+    swap_h.finish()
+    for block in range(RIM, BLOCKS):
+        descend(block, sums[plan[IN_LAST, block]])
+
+    share_second.wait_send()
+    share_inner = share(
+        4, all_of(first_delta, RIM, BLOCKS), all_of(other_first, RIM, BLOCKS)
+    )
 
     pl.semaphore_wait(reach.at[2], 2)
     back_h.arrive()

time: 65.8 us -> 65.1 us (0.989)
  the two profiles are of different devices: /device:TPU:257 before, /device:TPU:1 now
where the time goes in v8:
time: 65.1 us; the launch traced here: 63.9 us
  Pallas kernels  63.3 us (97%)
    pallas_call x1, Pallas kernels, shards(): pl.pallas_call(functools.partial(block_kernel, scale), out_shape=(field,...  61.9 us
    pallas_call x1, Pallas kernels, shards(): pl.pallas_call(lambda *refs: place_kernel(refs[0], refs[1], refs[2].at[pl...  1.33 us

profile of v8, /device:TPU:1, one launch (start us, length us, event | category | flops | bytes accessed | tf_op | source)
XLA Modules:
  0.0 63.9 jit_solution(14517339977723735504)
XLA Ops:
  0.6 61.9 %block.1 = (bf16[8,64,128]{2,1,0:T(8,128)(2,1)S(1)}, bf16[8,64,128]{2,1,0:T(8,128)(2,1)S(1)}, bf16[3584,128]{1,0:T(8,128)(2,1)S(1)}, bf16[3584,128]{1,0:T(8,128)(2,1)S(1)}) custom-call(bf16[8,64,128]{2,1,0:T(8,128)(2,1)} %bitcast.17, bf16[27,128,128]{2,1,0:T(8,128)(2,1)} %first_weight_in.1, bf16[27,128,128]{2,1,0:T(8,128)(2,1)} %second_weight_in.1, ...), custom_call_target="tpu_custom_call" | custom-call | flops 679477248 | bytes 3670016 | tf_op jit(solution)/shard_map/block/pallas_call | solution.py:634
  62.6 1.3 %place.1 = (bf16[8,64,128]{2,1,0:T(8,128)(2,1)}, bf16[8,64,128]{2,1,0:T(8,128)(2,1)}, bf16[3456,128]{1,0:T(8,128)(2,1)}, bf16[3456,128]{1,0:T(8,128)(2,1)}) custom-call(bf16[8,64,128]{2,1,0:T(8,128)(2,1)S(1)} %get-tuple-element.12.refs_0_, bf16[8,64,128]{2,1,0:T(8,128)(2,1)S(1)} %get-tuple-element.13.refs_1_, ...), custom_call_target="tpu_custom_call" | custom-call | tf_op jit(solution)/shard_map/place/pallas_call | solution.py:661

commit v9 on v8

--- a/solution.py
+++ b/solution.py
@@ -16,6 +16,7 @@
 FULL = 2 * HALF
 HALF_OFFSETS = HALF // 128
 PIECE = HALF // 16
+CHUNKS = ((0, 64), (64, 48))
 
 
 def rows(start, size):
@@ -76,25 +77,22 @@
 
 
 class Reduce:
-    scratch = [
-        pltpu.VMEM((HALF, 128), jnp.bfloat16),
-        pltpu.VMEM((15, PIECE, 128), jnp.bfloat16),
-        pltpu.VMEM((PIECE, 128), jnp.bfloat16),
-        pltpu.VMEM((15, PIECE, 128), jnp.bfloat16),
-        pltpu.SemaphoreType.DMA((5,)),
-        pltpu.SemaphoreType.DMA((8,)),
-    ]
-
-    def __init__(self, out, scale, *scratch):
-        self.out, self.scale = out, scale
-        (
-            self.part,
-            self.got_plane,
-            self.plane_sum,
-            self.got_root,
-            self.send_sems,
-            self.recv_sems,
-        ) = scratch
+    @staticmethod
+    def scratch(size):
+        return [
+            pltpu.VMEM((15, size, 128), jnp.bfloat16),
+            pltpu.VMEM((size, 128), jnp.bfloat16),
+            pltpu.VMEM((15, size, 128), jnp.bfloat16),
+            pltpu.SemaphoreType.DMA((5,)),
+            pltpu.SemaphoreType.DMA((8,)),
+        ]
+
+    def __init__(self, part, out, scale, offset, size, scratch):
+        self.part, self.out, self.scale, self.offset, self.size = part, out, scale, offset, size
+        self.got_plane, self.plane_sum, self.got_root, self.send_sems, self.recv_sems = scratch
+
+    def piece(self, d):
+        return rows(plane_index(d) * PIECE + self.offset, self.size)
 
     def send(self, src, dst, send_index, recv_index, device_id):
         pltpu.make_async_remote_copy(
@@ -106,13 +104,13 @@
             device_id_type=MESH,
         ).start()
 
-    def sent(self, index, count, size):
-        wait_bytes(self.part.at[pl.ds(0, count * size)], self.send_sems.at[index])
+    def sent(self, index, count):
+        wait_bytes(self.part.at[pl.ds(0, count * self.size)], self.send_sems.at[index])
 
     def start_plane(self):
         for d in PLANE:
             self.send(
-                self.part.at[rows(plane_index(d) * PIECE, PIECE)],
+                self.part.at[self.piece(d)],
                 self.got_plane.at[d - 1],
                 0,
                 0,
@@ -121,7 +119,7 @@
 
     def start_root(self):
         wait_bytes(self.got_plane, self.recv_sems.at[0])
-        total = self.part[rows(plane_index(0) * PIECE, PIECE)].astype(jnp.float32)
+        total = self.part[self.piece(0)].astype(jnp.float32)
         for d in range(15):
             total = total + self.got_plane[d].astype(jnp.float32)
         self.plane_sum[...] = total.astype(jnp.bfloat16)
@@ -131,10 +129,12 @@
         def _():
             self.send(self.plane_sum, self.got_root.at[z - 1], 1, 1, device(0, x, y, core))
 
-        self.sent(0, 15, PIECE)
+        self.sent(0, 15)
 
     def spot(self, d, core):
-        return self.out.at[rows(core * HALF + plane_index(d) * PIECE, PIECE)]
+        return self.out.at[
+            rows(core * HALF + plane_index(d) * PIECE + self.offset, self.size)
+        ]
 
     def start_spread(self):
         z, x, y, core = place()
@@ -155,7 +155,7 @@
 
         @pl.when(z > 0)
         def _():
-            self.sent(1, 1, PIECE)
+            self.sent(1, 1)
             wait_bytes(own, self.recv_sems.at[2])
 
         for d in PLANE:
@@ -168,22 +168,22 @@
 
     def start_core(self):
         core = place()[3]
-        for index in range(4):
+        for index in (3, 2, 1, 0):
             group = [d for d in PLANE if ring_of(d) == index]
-            wait_bytes(self.part.at[pl.ds(0, len(group) * PIECE)], self.recv_sems.at[3 + index])
+            wait_bytes(self.part.at[pl.ds(0, len(group) * self.size)], self.recv_sems.at[3 + index])
             for d in group:
                 piece = self.spot(opposite(d), core)
                 self.send(piece, piece, 4, 7, partner())
 
         @pl.when(place()[0] == 0)
         def _():
-            self.sent(2, 15, PIECE)
-
-        self.sent(3, 15, PIECE)
+            self.sent(2, 15)
+
+        self.sent(3, 15)
 
     def finish(self):
-        wait_bytes(self.part, self.recv_sems.at[7])
-        self.sent(4, 16, PIECE)
+        wait_bytes(self.part.at[pl.ds(0, 16 * self.size)], self.recv_sems.at[7])
+        self.sent(4, 16)
 
 
 def greet(peers):
@@ -386,6 +386,8 @@
     pltpu.SemaphoreType.DMA((7,)),
     pltpu.SemaphoreType.DMA((2, 4)),
     pltpu.SemaphoreType.REGULAR((3,)),
+    pltpu.VMEM((HALF, 128), jnp.bfloat16),
+    pltpu.VMEM((HALF, 128), jnp.bfloat16),
 ]
 
 
@@ -431,11 +433,16 @@
         core_sems,
         swap_sems,
         reach,
+        first_part,
+        second_part,
     ) = scratch[: len(SCRATCH)]
-    count = len(Reduce.scratch)
     reduces = scratch[len(SCRATCH) :]
-    first = Reduce(first_grad, scale, *reduces[:count])
-    second = Reduce(second_grad, scale, *reduces[count:])
+    first = [
+        Reduce(first_part, first_grad, scale, *chunk, reduces[5 * n : 5 * n + 5])
+        for n, chunk in enumerate(CHUNKS)
+    ]
+    second = Reduce(second_part, second_grad, scale, 0, PIECE, reduces[5 * len(CHUNKS) :])
+
 
     def load(index, src, dst):
         copy = pltpu.make_async_copy(src, dst, load_sems.at[index])
@@ -556,7 +563,7 @@
     share_h.wait_recv()
     share_second.wait_recv()
     weight_terms(
-        (table_h, other_h), (second_delta, other_second), (plan, other_plan), second.part
+        (table_h, other_h), (second_delta, other_second), (plan, other_plan), second_part
     )
     second.start_plane()
     swap_h.finish()
@@ -577,8 +584,9 @@
     share_x.wait_recv()
     share_inner.wait_recv()
     share_rim.wait_recv()
-    weight_terms((table_x, other_x), (first_delta, other_first), (plan, other_plan), first.part)
-    first.start_plane()
+    weight_terms((table_x, other_x), (first_delta, other_first), (plan, other_plan), first_part)
+    for chunk in first:
+        chunk.start_plane()
 
     second.start_root()
     back_h.finish()
@@ -586,7 +594,8 @@
     def land(block, total):
         input_grad[block] = (total + second_delta[block].astype(jnp.float32)).astype(jnp.bfloat16)
 
-    first.start_root()
+    for chunk in first:
+        chunk.start_root()
     convolve(first_delta, plan, DELTA, IN_CHAIN, first_weight, sums, True)
     give(give_x)
     back_x = Swap(3, swap_sems, eight(give_x), eight(got_x), got_x)
@@ -598,11 +607,14 @@
         land(r, routed(sums[plan[IN_LAST, r]], got_x, r))
     share_rim.wait_send()
     back_x.finish()
-    first.start_spread()
+    for chunk in first:
+        chunk.start_spread()
     second.start_core()
+    for chunk in first:
+        chunk.start_core()
     second.finish()
-    first.start_core()
-    first.finish()
+    for chunk in first:
+        chunk.finish()
 
 
 def place_kernel(*refs):
@@ -636,7 +648,9 @@
         out_shape=(field, field, grad, grad),
         in_specs=[hbm] * 7,
         out_specs=[vmem] * 4,
-        scratch_shapes=SCRATCH + Reduce.scratch * 2,
+        scratch_shapes=SCRATCH
+        + [shape for _, size in CHUNKS for shape in Reduce.scratch(size)]
+        + Reduce.scratch(PIECE),
         compiler_params=pltpu.CompilerParams(
             collective_id=0, has_side_effects=True, vmem_limit_bytes=48 * 1024 * 1024
         ),

time: 65.1 us -> 65.5 us (level)
    pallas_call x1, Pallas kernels: 61.9 us -> 62.6 us  [shards(): pl.pallas_call(functools.partial(block_kernel, scale), out_shape=(field,...]
where the time goes in v9:
time: 65.5 us; the launch traced here: 64.6 us
  Pallas kernels  63.9 us (98%)
    pallas_call x1, Pallas kernels, shards(): pl.pallas_call(functools.partial(block_kernel, scale), out_shape=(field,...  62.6 us
    pallas_call x1, Pallas kernels, shards(): pl.pallas_call(lambda *refs: place_kernel(refs[0], refs[1], refs[2].at[pl...  1.33 us

profile of v9, /device:TPU:1, one launch (start us, length us, event | category | flops | bytes accessed | tf_op | source)
XLA Modules:
  0.0 64.6 jit_solution(14943887907164772173)
XLA Ops:
  0.6 62.6 %block.1 = (bf16[8,64,128]{2,1,0:T(8,128)(2,1)S(1)}, bf16[8,64,128]{2,1,0:T(8,128)(2,1)S(1)}, bf16[3584,128]{1,0:T(8,128)(2,1)S(1)}, bf16[3584,128]{1,0:T(8,128)(2,1)S(1)}) custom-call(bf16[8,64,128]{2,1,0:T(8,128)(2,1)} %bitcast.17, bf16[27,128,128]{2,1,0:T(8,128)(2,1)} %first_weight_in.1, bf16[27,128,128]{2,1,0:T(8,128)(2,1)} %second_weight_in.1, ...), custom_call_target="tpu_custom_call" | custom-call | flops 679477248 | bytes 3670016 | tf_op jit(solution)/shard_map/block/pallas_call | solution.py:646
  63.2 1.3 %place.1 = (bf16[8,64,128]{2,1,0:T(8,128)(2,1)}, bf16[8,64,128]{2,1,0:T(8,128)(2,1)}, bf16[3456,128]{1,0:T(8,128)(2,1)}, bf16[3456,128]{1,0:T(8,128)(2,1)}) custom-call(bf16[8,64,128]{2,1,0:T(8,128)(2,1)S(1)} %get-tuple-element.12.refs_0_, bf16[8,64,128]{2,1,0:T(8,128)(2,1)S(1)} %get-tuple-element.13.refs_1_, ...), custom_call_target="tpu_custom_call" | custom-call | tf_op jit(solution)/shard_map/place/pallas_call | solution.py:675

commit v10 on v8

--- a/solution.py
+++ b/solution.py
@@ -168,7 +168,7 @@
 
     def start_core(self):
         core = place()[3]
-        for index in range(4):
+        for index in (3, 2, 1, 0):
             group = [d for d in PLANE if ring_of(d) == index]
             wait_bytes(self.part.at[pl.ds(0, len(group) * PIECE)], self.recv_sems.at[3 + index])
             for d in group:
@@ -600,8 +600,8 @@
     back_x.finish()
     first.start_spread()
     second.start_core()
+    first.start_core()
     second.finish()
-    first.start_core()
     first.finish()
 
 

time: 65.1 us -> 65.2 us (level)
  no operation moved by 1% of the time
where the time goes in v10:
time: 65.2 us; the launch traced here: 64.1 us
  Pallas kernels  63.5 us (97%)
    pallas_call x1, Pallas kernels, shards(): pl.pallas_call(functools.partial(block_kernel, scale), out_shape=(field,...  62.2 us
    pallas_call x1, Pallas kernels, shards(): pl.pallas_call(lambda *refs: place_kernel(refs[0], refs[1], refs[2].at[pl...  1.33 us

profile of v10, /device:TPU:1, one launch (start us, length us, event | category | flops | bytes accessed | tf_op | source)
XLA Modules:
  0.0 64.1 jit_solution(8852100580301061979)
XLA Ops:
  0.6 62.2 %block.1 = (bf16[8,64,128]{2,1,0:T(8,128)(2,1)S(1)}, bf16[8,64,128]{2,1,0:T(8,128)(2,1)S(1)}, bf16[3584,128]{1,0:T(8,128)(2,1)S(1)}, bf16[3584,128]{1,0:T(8,128)(2,1)S(1)}) custom-call(bf16[8,64,128]{2,1,0:T(8,128)(2,1)} %bitcast.17, bf16[27,128,128]{2,1,0:T(8,128)(2,1)} %first_weight_in.1, bf16[27,128,128]{2,1,0:T(8,128)(2,1)} %second_weight_in.1, ...), custom_call_target="tpu_custom_call" | custom-call | flops 679477248 | bytes 3670016 | tf_op jit(solution)/shard_map/block/pallas_call | solution.py:634
  62.8 1.3 %place.1 = (bf16[8,64,128]{2,1,0:T(8,128)(2,1)}, bf16[8,64,128]{2,1,0:T(8,128)(2,1)}, bf16[3456,128]{1,0:T(8,128)(2,1)}, bf16[3456,128]{1,0:T(8,128)(2,1)}) custom-call(bf16[8,64,128]{2,1,0:T(8,128)(2,1)S(1)} %get-tuple-element.12.refs_0_, bf16[8,64,128]{2,1,0:T(8,128)(2,1)S(1)} %get-tuple-element.13.refs_1_, ...), custom_call_target="tpu_custom_call" | custom-call | tf_op jit(solution)/shard_map/place/pallas_call | solution.py:661
